TPU v7x, 32 devices: a whole 2x2x4 slice. The times are simulated.
32 devices in a mesh: dp: 16 (over z, y, core), tensor: 2 (over x).
Axes of the slice: x: 2, y: 2, z: 4, core: 2. Of those that a mesh axis runs over, the one named last changes fastest.
Arguments:
- acts: bfloat16 [16384, 8192], P('dp', 'tensor'), may hold values from -6 to 6
- out_grads: bfloat16 [16384, 28672], P('dp', 'tensor'), may hold values from -6 to 6
- proj_in: bfloat16 [64, 8192], P(None, 'tensor'), may hold values from -0.0625 to 0.0625
- proj_out: bfloat16 [64, 28672], P(None, 'tensor'), may hold values from -0.03125 to 0.03125
- lengths: int32 [64], P('dp'), may hold values from 1 to 256, 8192 in all
- queries: float32 [512, 4096], P('tensor', 'dp'), may hold values from -6 to 6
- query_ids: int32 [512], P('tensor'), may hold values from 0 to 63
Outputs:
- scores: float32 [64, 512], P('dp', 'tensor')
All inputs are finite; a program needn't handle non-finite values. No bound on the sum of `lengths` on one device may be relied on, other than what follows from the above.
Results may differ from a plain program's by a relative error of at most 0.0003.
Values sent between devices are 32-bit elements; how exact they have to be, the bound alone decides.
No kernel may reach another device: no remote copies, remote signals or barrier semaphores. Data moves between devices by JAX's collectives and lax.ppermute only.
A program may use at most 128 MiB of HBM per device.

v0:
```python
import functools

import jax
import jax.numpy as jnp
from jax import lax
from jax.experimental import pallas as pl
from jax.experimental.pallas import tpu as pltpu
from jax.sharding import PartitionSpec as P

BLOCK = 64
NEAR_BITS = 3
NT = (((1,), (1,)), ((), ()))
TN = (((0,), (0,)), ((), ()))
HBM = pl.BlockSpec(memory_space=pltpu.HBM)
VMEM = pl.BlockSpec(memory_space=pltpu.VMEM)


def xor_pairs(size, mask):
    return [(i, i ^ mask) for i in range(size)]


def swap(x, mask):
    return lax.ppermute(x, "dp", xor_pairs(lax.axis_size("dp"), mask))


def project_kernel(peer, count, slot, lengths, acts, grads, proj_in, proj_out, out,
                   used, act_buf, grad_buf, in_buf, out_buf, sems, small):
    per = slot // BLOCK
    blocks = count * per
    first = 0
    if peer is not None:
        mine = lax.axis_index("tensor")
        first = (1 - mine if peer else mine) * count
    rank = proj_out.shape[0]

    def copies(j):
        row = pl.multiple_of(first * slot + j * BLOCK, BLOCK)
        return (
            pltpu.make_async_copy(grads.at[pl.ds(row, BLOCK)], grad_buf.at[j], sems.at[0, j]),
            pltpu.make_async_copy(acts.at[pl.ds(row, BLOCK)], act_buf.at[j], sems.at[1, j]),
        )

    def left(j):
        return used[first + j // per] - (j % per) * BLOCK

    get_used = pltpu.make_async_copy(lengths, used, small.at[0])
    get_out = pltpu.make_async_copy(proj_out, out_buf, small.at[1])
    get_in = pltpu.make_async_copy(proj_in, in_buf, small.at[2])
    get_used.start()
    get_out.start()
    for copy in copies(0):
        copy.start()
    get_in.start()
    get_used.wait()

    @pl.loop(1, blocks)
    def _(j):
        @pl.when(left(j) > 0)
        def _():
            for copy in copies(j):
                copy.start()

    get_out.wait()
    get_in.wait()

    @pl.loop(0, blocks)
    def _(j):
        rows = left(j)

        @pl.when(rows > 0)
        def _():
            for copy in copies(j):
                copy.wait()
            part_grads = lax.dot_general(
                grad_buf[j], out_buf[...], NT, preferred_element_type=jnp.float32
            )
            part_acts = lax.dot_general(
                act_buf[j], in_buf[...], NT, preferred_element_type=jnp.float32
            )
            joined = jnp.concatenate([part_grads, part_acts], axis=1)
            row = lax.broadcasted_iota(jnp.int32, joined.shape, 0)
            out[j] = jnp.where(row < rows, joined, 0.0)

        @pl.when(rows <= 0)
        def _():
            out[j] = jnp.zeros((BLOCK, 2 * rank), jnp.float32)


def project(peer, count, slot, *args):
    lengths, acts, grads, proj_in, proj_out = args
    blocks = count * slot // BLOCK
    width = proj_out.shape[0] + proj_in.shape[0]
    rows = blocks * BLOCK
    depth = acts.shape[1] + grads.shape[1]
    return pl.pallas_call(
        functools.partial(project_kernel, peer, count, slot),
        out_shape=jax.ShapeDtypeStruct((blocks, BLOCK, width), jnp.float32),
        in_specs=[HBM] * 5,
        out_specs=VMEM,
        scratch_shapes=[
            pltpu.SMEM(lengths.shape, jnp.int32),
            pltpu.VMEM((blocks, BLOCK, acts.shape[1]), acts.dtype),
            pltpu.VMEM((blocks, BLOCK, grads.shape[1]), grads.dtype),
            pltpu.VMEM(proj_in.shape, proj_in.dtype),
            pltpu.VMEM(proj_out.shape, proj_out.dtype),
            pltpu.SemaphoreType.DMA((2, blocks)),
            pltpu.SemaphoreType.DMA((3,)),
        ],
        compiler_params=pltpu.CompilerParams(
            vmem_limit_bytes=2 * (rows + width) * depth + (6 << 20)
        ),
        cost_estimate=pl.CostEstimate(
            flops=width * rows * depth, bytes_accessed=2 * rows * depth, transcendentals=0
        ),
        name="project",
    )(*[pltpu.with_memory_space_constraint(x, pltpu.HBM) for x in args])


def hi_lo(x):
    hi = x.astype(jnp.bfloat16)
    return hi, (x - hi.astype(jnp.float32)).astype(jnp.bfloat16)


def unit_kernel(count, rank, near, rest, *refs):
    parts, out, square, cols = refs[:-3], refs[-3], refs[-2], refs[-1]
    here = lax.axis_index("dp")
    split, per = cols.shape[1], square.shape[1] // cols.shape[1]
    for e in range(count):
        total = parts[0][e]
        for part in parts[1:]:
            total = total + part[e]
        grads = jnp.concatenate(hi_lo(total[:, :rank]), axis=1)
        acts = jnp.concatenate(hi_lo(total[:, rank:]), axis=1)
        both = lax.dot_general(grads, acts, TN, preferred_element_type=jnp.float32)
        width = total.shape[1] - rank
        kron = (both[:rank, :width] + both[rank:, width:]) + (
            both[:rank, width:] + both[rank:, :width]
        )
        norm = jnp.sqrt(jnp.sum(kron * kron, keepdims=True) + 1e-06)
        square[e] = kron / norm
        cols[e] = jnp.concatenate(
            [square[e, pl.ds(c, split, stride=per), :] for c in range(per)], axis=1
        )
        for g, r in enumerate(rest):
            for k, m in enumerate(near):
                out[g, e, k : k + 1] = cols[e, pl.ds(here ^ (r ^ m), 1), :]


def units(parts, count, slot, rank, split, near, rest):
    width = parts[0].shape[-1]
    piece = rank * (width - rank) // split
    parts = [part.reshape(count, slot, width) for part in parts]
    return pl.pallas_call(
        functools.partial(unit_kernel, count, rank, near, rest),
        out_shape=jax.ShapeDtypeStruct((len(rest), count, len(near), piece), jnp.float32),
        in_specs=[VMEM] * len(parts),
        out_specs=VMEM,
        scratch_shapes=[
            pltpu.VMEM((count, rank, width - rank), jnp.float32),
            pltpu.VMEM((count, split, piece), jnp.float32),
        ],
        compiler_params=pltpu.CompilerParams(vmem_limit_bytes=8 << 20),
        name="units",
    )(*parts)


def score_kernel(sources, halves, *refs):
    rows_of, blocks, outs = refs[:sources], refs[sources:-sources], refs[-sources:]
    count = rows_of[0].shape[0]
    rows_all = count * sources
    total = jnp.zeros((rows_all, outs[0].shape[1]), jnp.float32)
    for m, block in enumerate(blocks):
        rows = jnp.concatenate(
            [ref[e, m : m + 1, :] for ref in rows_of for e in range(count)], axis=0
        )
        rows_hi, rows_lo = hi_lo(rows)
        block_hi, block_lo = hi_lo(block[...])
        both = lax.dot_general(
            jnp.concatenate([rows_hi, rows_lo], axis=0), block_hi, NT,
            preferred_element_type=jnp.float32,
        )
        cross = lax.dot_general(rows_hi, block_lo, NT, preferred_element_type=jnp.float32)
        total = total + (both[:rows_all] + (both[rows_all:] + cross))
    for g, out in enumerate(outs):
        mine = total[g * count : (g + 1) * count]
        if halves:
            turned = jnp.concatenate([mine[count // 2 :], mine[: count // 2]], axis=0)
            mine = jnp.where(lax.axis_index("tensor") == 1, turned, mine)
        out[...] = mine


def partial_scores(rows_of, blocks, halves):
    sources = len(rows_of)
    shape = jax.ShapeDtypeStruct((rows_of[0].shape[0], blocks[0].shape[0]), jnp.float32)
    return pl.pallas_call(
        functools.partial(score_kernel, sources, halves),
        out_shape=[shape] * sources,
        in_specs=[VMEM] * (sources + len(blocks)),
        out_specs=[VMEM] * sources,
        compiler_params=pltpu.CompilerParams(vmem_limit_bytes=16 << 20),
        name="scores",
    )(*rows_of, *blocks)


def span(bits):
    masks = [0]
    for bit in bits:
        masks = masks + [m ^ bit for m in masks]
    return masks


def on_device(acts, out_grads, proj_in, proj_out, lengths, queries, query_ids):
    rank_out = proj_out.shape[0]
    ex_count = lengths.shape[0]
    slot = acts.shape[0] // ex_count
    split = lax.axis_size("dp")
    bits = [1 << i for i in range(split.bit_length() - 1)]
    near = span(bits[:NEAR_BITS])
    rest = span(bits[NEAR_BITS:])
    halves = lax.axis_size("tensor") == 2 and ex_count % 2 == 0
    args = (lengths, acts, out_grads, proj_in, proj_out)
    blocks = {0: queries}
    for m in near:
        if m == 1 or m % 2 == 0 and m > 0:
            blocks[m] = swap(queries, m)
    if halves:
        count = ex_count // 2
        theirs = project(True, count, slot, *args)
        arrived = lax.ppermute(theirs, "tensor", [(0, 1), (1, 0)])
        parts = [project(False, count, slot, *args), arrived]
    else:
        count = ex_count
        parts = [lax.psum(project(None, count, slot, *args), "tensor")]
    early = {m: blocks[m] for m in blocks if m < 6}
    early, parts = lax.optimization_barrier((early, parts))
    blocks = {**blocks, **early}
    own = units(parts, count, slot, rank_out, split, near, rest)
    if halves:
        own = jnp.concatenate([own, lax.ppermute(own, "tensor", [(0, 1), (1, 0)])], axis=1)
        own, blocks = lax.optimization_barrier((own, blocks))
    rows_of = [own[g] if r == 0 else swap(own[g], r) for g, r in enumerate(rest)]
    for m in near:
        if m > 1 and m % 2 == 1:
            blocks[m] = swap(blocks[m ^ 1], 1)
    sums = partial_scores(rows_of, [blocks[m] for m in near], halves)
    scores = sums[0]
    for r, got in zip(rest[1:], sums[1:]):
        scores = scores + swap(got, r)
    example_ids = lax.axis_index("dp") * ex_count + lax.broadcasted_iota(
        jnp.int32, (ex_count, 1), 0
    )
    same = example_ids == query_ids[None, :]
    return jnp.where(same, jnp.zeros_like(scores), scores)


def solution(mesh):
    in_specs = (
        P("dp", "tensor"),
        P("dp", "tensor"),
        P(None, "tensor"),
        P(None, "tensor"),
        P("dp"),
        P("tensor", "dp"),
        P("tensor"),
    )
    out_specs = P("dp", "tensor")
    return jax.shard_map(
        on_device, mesh=mesh, in_specs=in_specs, out_specs=out_specs, check_vma=False
    )
```

profile of v0, /device:TPU:0, one launch (start us, length us, event | category | flops | bytes accessed | tf_op | source)
XLA Modules:
  0.0 39.6 jit_solution(4779394683109638585)
XLA Ops:
  0.0 0.0 copy-start
  0.0 0.5 %collective-permute-start = (f32[256,256]{1,0:T(8,128)}, f32[256,256]{1,0:T(8,128)S(1)}, u32[]{:S(2)}, u32[]{:S(2)}) collective-permute-start(f32[256,256]{1,0:T(8,128)} %refs_2_), channel_id=1, source_target_pairs={{0,2},{2,0},{4,6},{6,4},{8,10},{10,8},{12,14},{14,12},{16,18},{18,... | collective-permute-start | bytes 786440 | tf_op jit(solution)/shard_map/ppermute | solution.py:23
  0.5 2.6 %collective-permute-start.1 = (f32[256,256]{1,0:T(8,128)}, f32[256,256]{1,0:T(8,128)S(1)}, u32[]{:S(2)}, u32[]{:S(2)}) collective-permute-start(f32[256,256]{1,0:T(8,128)} %refs_2_), channel_id=1, source_target_pairs={{0,4},{2,6},{4,0},{6,2},{8,12},{10,14},{12,8},{14,10},{16,20},{18,... | collective-permute-start | bytes 786440 | tf_op jit(solution)/shard_map/ppermute | solution.py:23
  3.0 1.6 %collective-permute-start.2 = (f32[256,256]{1,0:T(8,128)}, f32[256,256]{1,0:T(8,128)S(1)}, u32[]{:S(2)}, u32[]{:S(2)}) collective-permute-start(f32[256,256]{1,0:T(8,128)} %refs_2_), channel_id=1, source_target_pairs={{0,8},{2,10},{4,12},{6,14},{8,0},{10,2},{12,4},{14,6},{16,24},{18,... | collective-permute-start | bytes 786440 | tf_op jit(solution)/shard_map/ppermute | solution.py:23
  4.6 5.9 %project.3 = f32[8,64,128]{2,1,0:T(8,128)S(1)} custom-call(s32[4]{0:T(128)} %lengths.3, bf16[1024,4096]{1,0:T(8,128)(2,1)} %acts.3, bf16[1024,14336]{1,0:T(8,128)(2,1)} %grads.3, bf16[64,4096]{1,0:T(8,128)(2,1)} %proj_in.3, bf16[64,14336]{1,0:T(8,128)(2,1)} %proj_out.3), custom_call_target="tpu_custom_call" | custom-call | flops 1207959552 | bytes 18874368 | tf_op jit(solution)/shard_map/project/pallas_call | solution.py:95
  10.6 0.0 copy-start.1
  10.6 0.7 %collective-permute-start.3 = (f32[8,64,128]{2,1,0:T(8,128)S(1)}, f32[8,64,128]{2,1,0:T(8,128)S(1)}, u32[]{:S(2)}, u32[]{:S(2)}) collective-permute-start(f32[8,64,128]{2,1,0:T(8,128)S(1)} %project.3), channel_id=1, source_target_pairs={{0,1},{1,0},{2,3},{3,2},{4,5},{5,4},{6,7},{7,6},{8,9},{9,8},{10,11... | collective-permute-start | bytes 786440 | tf_op jit(solution)/shard_map/ppermute | solution.py:229
  11.3 0.0 copy-done
  11.3 2.9 %collective-permute-start.5 = (f32[256,256]{1,0:T(8,128)S(1)}, f32[256,256]{1,0:T(8,128)S(1)}, u32[]{:S(2)}, u32[]{:S(2)}) collective-permute-start(f32[256,256]{1,0:T(8,128)S(1)} %copy-done), channel_id=1, source_target_pairs={{0,12},{2,14},{4,8},{6,10},{8,4},{10,6},{12,0},{14,2},{16,28},{18,... | collective-permute-start | bytes 786440 | tf_op jit(solution)/shard_map/ppermute | solution.py:23
  14.2 5.1 %project.2 = f32[8,64,128]{2,1,0:T(8,128)S(1)} custom-call(s32[4]{0:T(128)} %lengths.3, bf16[1024,4096]{1,0:T(8,128)(2,1)} %acts.3, bf16[1024,14336]{1,0:T(8,128)(2,1)} %grads.3, bf16[64,4096]{1,0:T(8,128)(2,1)} %proj_in.3, bf16[64,14336]{1,0:T(8,128)(2,1)} %proj_out.3), custom_call_target="tpu_custom_call" | custom-call | flops 1207959552 | bytes 18874368 | tf_op jit(solution)/shard_map/project/pallas_call | solution.py:95
  19.3 0.0 collective-permute-done.refs_3_
  19.3 0.0 collective-permute-done.1.refs_4_
  19.3 0.0 collective-permute-done.2.refs_6_
  19.3 0.0 collective-permute-done.3
  19.3 0.7 %units.1 = f32[2,2,8,256]{3,2,1,0:T(8,128)S(1)} custom-call(f32[2,256,128]{2,1,0:T(8,128)S(1)} %bitcast.6, f32[2,256,128]{2,1,0:T(8,128)S(1)} %bitcast.7), custom_call_target="tpu_custom_call" | custom-call | tf_op jit(solution)/shard_map/units/pallas_call | solution.py:153
  20.0 1.9 %collective-permute-start.4 = (f32[2,2,8,256]{3,2,1,0:T(8,128)S(1)}, f32[2,2,8,256]{3,2,1,0:T(8,128)S(1)}, u32[]{:S(2)}, u32[]{:S(2)}) collective-permute-start(f32[2,2,8,256]{3,2,1,0:T(8,128)S(1)} %units.1), channel_id=1, source_target_pairs={{0,1},{1,0},{2,3},{3,2},{4,5},{5,4},{6,7},{7,6},{8,9},{9,8},{10,11... | collective-permute-start | bytes 98312 | tf_op jit(solution)/shard_map/ppermute | solution.py:239
  21.9 2.1 %collective-permute-done.4 = f32[2,2,8,256]{3,2,1,0:T(8,128)S(1)} collective-permute-done((f32[2,2,8,256]{3,2,1,0:T(8,128)S(1)}, f32[2,2,8,256]{3,2,1,0:T(8,128)S(1)}, u32[]{:S(2)}, u32[]{:S(2)}) %collective-permute-start.4) | collective-permute-done | bytes 32800 | tf_op jit(solution)/shard_map/ppermute | solution.py:239
  24.0 0.0 collective-permute-done.5.refs_8_
  24.0 1.5 %collective-permute-start.7 = (f32[256,256]{1,0:T(8,128)S(1)}, f32[256,256]{1,0:T(8,128)S(1)}, u32[]{:S(2)}, u32[]{:S(2)}) collective-permute-start(f32[256,256]{1,0:T(8,128)S(1)} %collective-permute-done.1.refs_4_), channel_id=1, source_target_pairs={{0,2},{2,0},{4,6},{6,4},{8,10},{10,8},{12,14},{14,12},{16,18},{18,... | collective-permute-start | bytes 786440 | tf_op jit(solution)/shard_map/ppermute | solution.py:23
  25.5 0.1 collective-permute-start.8
  25.6 0.4 %collective-permute-start.9 = (f32[256,256]{1,0:T(8,128)S(1)}, f32[256,256]{1,0:T(8,128)S(1)}, u32[]{:S(2)}, u32[]{:S(2)}) collective-permute-start(f32[256,256]{1,0:T(8,128)S(1)} %collective-permute-done.5.refs_8_), channel_id=1, source_target_pairs={{0,2},{2,0},{4,6},{6,4},{8,10},{10,8},{12,14},{14,12},{16,18},{18,... | collective-permute-start | bytes 786440 | tf_op jit(solution)/shard_map/ppermute | solution.py:23
  26.1 4.9 %collective-permute-start.6 = (f32[4,8,256]{2,1,0:T(8,128)S(1)}, f32[4,8,256]{2,1,0:T(8,128)S(1)}, u32[]{:S(2)}, u32[]{:S(2)}) collective-permute-start(f32[4,8,256]{2,1,0:T(8,128)S(1)} %get-tuple-element.33), channel_id=1, source_target_pairs={{0,16},{2,18},{4,20},{6,22},{8,24},{10,26},{12,28},{14,30},{16,0},... | collective-permute-start | bytes 98312 | tf_op jit(solution)/shard_map/ppermute | solution.py:23
  31.0 2.7 %collective-permute-done.6.refs_1_ = f32[4,8,256]{2,1,0:T(8,128)S(1)} collective-permute-done((f32[4,8,256]{2,1,0:T(8,128)S(1)}, f32[4,8,256]{2,1,0:T(8,128)S(1)}, u32[]{:S(2)}, u32[]{:S(2)}) %collective-permute-start.6) | collective-permute-done | bytes 32800 | tf_op jit(solution)/shard_map/ppermute | solution.py:23
  33.7 0.0 collective-permute-done.7.refs_5_
  33.7 0.0 collective-permute-done.8.refs_7_
  33.7 0.0 collective-permute-done.9.refs_9_
  33.7 0.6 %scores.1 = (f32[4,256]{1,0:T(4,128)S(1)}, f32[4,256]{1,0:T(4,128)S(1)}) custom-call(f32[4,8,256]{2,1,0:T(8,128)S(1)} %get-tuple-element.34.refs_0_, f32[4,8,256]{2,1,0:T(8,128)S(1)} %collective-permute-done.6.refs_1_, f32[256,256]{1,0:T(8,128)S(1)} %copy-done, f32[256,256]{1,0:T(8,128)S(1)} %collective-permute-done.refs_3_, ...), custom_call_target="tpu_custom_call" | custom-call | tf_op jit(solution)/shard_map/scores/pallas_call | solution.py:195
  34.3 2.2 %collective-permute-start.10 = (f32[4,256]{1,0:T(4,128)S(1)}, f32[4,256]{1,0:T(4,128)S(1)}, u32[]{:S(2)}, u32[]{:S(2)}) collective-permute-start(f32[4,256]{1,0:T(4,128)S(1)} %get-tuple-element.32), channel_id=1, source_target_pairs={{0,16},{2,18},{4,20},{6,22},{8,24},{10,26},{12,28},{14,30},{16,0},... | collective-permute-start | bytes 12296 | tf_op jit(solution)/shard_map/ppermute | solution.py:23
  36.5 2.4 %collective-permute-done.10 = f32[4,256]{1,0:T(4,128)S(1)} collective-permute-done((f32[4,256]{1,0:T(4,128)S(1)}, f32[4,256]{1,0:T(4,128)S(1)}, u32[]{:S(2)}, u32[]{:S(2)}) %collective-permute-start.10) | collective-permute-done | bytes 4128 | tf_op jit(solution)/shard_map/ppermute | solution.py:23
  38.9 0.0 copy-done.1
  38.9 0.7 %add_select_fusion = f32[4,256]{1,0:T(4,128)} fusion(f32[4,256]{1,0:T(4,128)S(1)} %get-tuple-element.31, f32[4,256]{1,0:T(4,128)S(1)} %collective-permute-done.10, s32[256]{0:T(256)S(1)} %copy-done.1, s32[4]{0:T(128)S(1)} %iota_add_fusion), kind=kLoop, calls=%fused_computation.3 | loop fusion | flops 3072 | bytes 13328 | tf_op jit(solution)/shard_map/jit(_where)/select_n | solution.py:253
  (3 shorter events, 0.0 us)
Async XLA Ops:
  0.0 11.3 %copy-start = (f32[256,256]{1,0:T(8,128)S(1)}, f32[256,256]{1,0:T(8,128)}, u32[]{:S(2)}) copy-start(f32[256,256]{1,0:T(8,128)} %refs_2_) | copy-start | bytes 786436
  0.0 19.3 %collective-permute-start = (f32[256,256]{1,0:T(8,128)}, f32[256,256]{1,0:T(8,128)S(1)}, u32[]{:S(2)}, u32[]{:S(2)}) collective-permute-start(f32[256,256]{1,0:T(8,128)} %refs_2_), channel_id=1, source_target_pairs={{0,2},{2,0},{4,6},{6,4},{8,10},{10,8},{12,14},{14,12},{16,18},{18,... | collective-permute-start | bytes 786440 | tf_op jit(solution)/shard_map/ppermute | solution.py:23
  0.5 18.8 %collective-permute-start.1 = (f32[256,256]{1,0:T(8,128)}, f32[256,256]{1,0:T(8,128)S(1)}, u32[]{:S(2)}, u32[]{:S(2)}) collective-permute-start(f32[256,256]{1,0:T(8,128)} %refs_2_), channel_id=1, source_target_pairs={{0,4},{2,6},{4,0},{6,2},{8,12},{10,14},{12,8},{14,10},{16,20},{18,... | collective-permute-start | bytes 786440 | tf_op jit(solution)/shard_map/ppermute | solution.py:23
  3.0 16.3 %collective-permute-start.2 = (f32[256,256]{1,0:T(8,128)}, f32[256,256]{1,0:T(8,128)S(1)}, u32[]{:S(2)}, u32[]{:S(2)}) collective-permute-start(f32[256,256]{1,0:T(8,128)} %refs_2_), channel_id=1, source_target_pairs={{0,8},{2,10},{4,12},{6,14},{8,0},{10,2},{12,4},{14,6},{16,24},{18,... | collective-permute-start | bytes 786440 | tf_op jit(solution)/shard_map/ppermute | solution.py:23
  10.6 28.4 %copy-start.1 = (s32[256]{0:T(256)S(1)}, s32[256]{0:T(256)}, u32[]{:S(2)}) copy-start(s32[256]{0:T(256)} %param.13) | copy-start | bytes 3076
  10.6 8.7 %collective-permute-start.3 = (f32[8,64,128]{2,1,0:T(8,128)S(1)}, f32[8,64,128]{2,1,0:T(8,128)S(1)}, u32[]{:S(2)}, u32[]{:S(2)}) collective-permute-start(f32[8,64,128]{2,1,0:T(8,128)S(1)} %project.3), channel_id=1, source_target_pairs={{0,1},{1,0},{2,3},{3,2},{4,5},{5,4},{6,7},{7,6},{8,9},{9,8},{10,11... | collective-permute-start | bytes 786440 | tf_op jit(solution)/shard_map/ppermute | solution.py:229
  11.3 12.7 %collective-permute-start.5 = (f32[256,256]{1,0:T(8,128)S(1)}, f32[256,256]{1,0:T(8,128)S(1)}, u32[]{:S(2)}, u32[]{:S(2)}) collective-permute-start(f32[256,256]{1,0:T(8,128)S(1)} %copy-done), channel_id=1, source_target_pairs={{0,12},{2,14},{4,8},{6,10},{8,4},{10,6},{12,0},{14,2},{16,28},{18,... | collective-permute-start | bytes 786440 | tf_op jit(solution)/shard_map/ppermute | solution.py:23
  20.0 4.0 %collective-permute-start.4 = (f32[2,2,8,256]{3,2,1,0:T(8,128)S(1)}, f32[2,2,8,256]{3,2,1,0:T(8,128)S(1)}, u32[]{:S(2)}, u32[]{:S(2)}) collective-permute-start(f32[2,2,8,256]{3,2,1,0:T(8,128)S(1)} %units.1), channel_id=1, source_target_pairs={{0,1},{1,0},{2,3},{3,2},{4,5},{5,4},{6,7},{7,6},{8,9},{9,8},{10,11... | collective-permute-start | bytes 98312 | tf_op jit(solution)/shard_map/ppermute | solution.py:239
  24.0 9.7 %collective-permute-start.7 = (f32[256,256]{1,0:T(8,128)S(1)}, f32[256,256]{1,0:T(8,128)S(1)}, u32[]{:S(2)}, u32[]{:S(2)}) collective-permute-start(f32[256,256]{1,0:T(8,128)S(1)} %collective-permute-done.1.refs_4_), channel_id=1, source_target_pairs={{0,2},{2,0},{4,6},{6,4},{8,10},{10,8},{12,14},{14,12},{16,18},{18,... | collective-permute-start | bytes 786440 | tf_op jit(solution)/shard_map/ppermute | solution.py:23
  25.5 8.1 %collective-permute-start.8 = (f32[256,256]{1,0:T(8,128)S(1)}, f32[256,256]{1,0:T(8,128)S(1)}, u32[]{:S(2)}, u32[]{:S(2)}) collective-permute-start(f32[256,256]{1,0:T(8,128)S(1)} %collective-permute-done.2.refs_6_), channel_id=1, source_target_pairs={{0,2},{2,0},{4,6},{6,4},{8,10},{10,8},{12,14},{14,12},{16,18},{18,... | collective-permute-start | bytes 786440 | tf_op jit(solution)/shard_map/ppermute | solution.py:23
  25.6 8.1 %collective-permute-start.9 = (f32[256,256]{1,0:T(8,128)S(1)}, f32[256,256]{1,0:T(8,128)S(1)}, u32[]{:S(2)}, u32[]{:S(2)}) collective-permute-start(f32[256,256]{1,0:T(8,128)S(1)} %collective-permute-done.5.refs_8_), channel_id=1, source_target_pairs={{0,2},{2,0},{4,6},{6,4},{8,10},{10,8},{12,14},{14,12},{16,18},{18,... | collective-permute-start | bytes 786440 | tf_op jit(solution)/shard_map/ppermute | solution.py:23
  26.1 7.6 %collective-permute-start.6 = (f32[4,8,256]{2,1,0:T(8,128)S(1)}, f32[4,8,256]{2,1,0:T(8,128)S(1)}, u32[]{:S(2)}, u32[]{:S(2)}) collective-permute-start(f32[4,8,256]{2,1,0:T(8,128)S(1)} %get-tuple-element.33), channel_id=1, source_target_pairs={{0,16},{2,18},{4,20},{6,22},{8,24},{10,26},{12,28},{14,30},{16,0},... | collective-permute-start | bytes 98312 | tf_op jit(solution)/shard_map/ppermute | solution.py:23
  34.3 4.6 %collective-permute-start.10 = (f32[4,256]{1,0:T(4,128)S(1)}, f32[4,256]{1,0:T(4,128)S(1)}, u32[]{:S(2)}, u32[]{:S(2)}) collective-permute-start(f32[4,256]{1,0:T(4,128)S(1)} %get-tuple-element.32), channel_id=1, source_target_pairs={{0,16},{2,18},{4,20},{6,22},{8,24},{10,26},{12,28},{14,30},{16,0},... | collective-permute-start | bytes 12296 | tf_op jit(solution)/shard_map/ppermute | solution.py:23
where the time goes:
time: 39.4 us; the launch traced here: 39.6 us
  starting transfers between devices  19.2 us (49%)
  Pallas kernels  12.4 us (31%)
  waiting for transfers between devices  7.2 us (18%)
  other arithmetic  0.67 us (2%)
    ppermute x9, starting transfers between devices, swap(): return lax.ppermute(x, 'dp', xor_pairs(lax.axis_size('dp'), mask))  16.6 us
    pallas_call x2, Pallas kernels, project(): pl.pallas_call(functools.partial(project_kernel, peer, count, slot), out_...  11.1 us
    ppermute x9, waiting for transfers between devices, swap(): return lax.ppermute(x, 'dp', xor_pairs(lax.axis_size('dp'), mask))  5.07 us
    ppermute x1, waiting for transfers between devices, on_device(): lax.ppermute(own, 'tensor', [(0, 1), (1, 0)])  2.12 us
    ppermute x1, starting transfers between devices, on_device(): lax.ppermute(own, 'tensor', [(0, 1), (1, 0)])  1.86 us
  transfers between devices with their start and end apart: 11, of which 3 were waited for; matrix products, arithmetic and copies ran while one was open for 0% of the time, Pallas kernels for 30%

commit v1 on v0

--- a/solution.py
+++ b/solution.py
@@ -23,15 +23,18 @@
     return lax.ppermute(x, "dp", xor_pairs(lax.axis_size("dp"), mask))
 
 
-def project_kernel(peer, count, slot, lengths, acts, grads, proj_in, proj_out, out,
-                   used, act_buf, grad_buf, in_buf, out_buf, sems, small):
+def project_kernel(peer, count, slot, held, lengths, acts, grads, *refs):
+    if held:
+        in_buf, out_buf, out, used, act_buf, grad_buf, sems, small = refs
+    else:
+        proj_in, proj_out, out, in_buf, out_buf, used, act_buf, grad_buf, sems, small = refs
     per = slot // BLOCK
     blocks = count * per
     first = 0
     if peer is not None:
         mine = lax.axis_index("tensor")
         first = (1 - mine if peer else mine) * count
-    rank = proj_out.shape[0]
+    rank = out_buf.shape[0]
 
     def copies(j):
         row = pl.multiple_of(first * slot + j * BLOCK, BLOCK)
@@ -44,13 +47,14 @@
         return used[first + j // per] - (j % per) * BLOCK
 
     get_used = pltpu.make_async_copy(lengths, used, small.at[0])
-    get_out = pltpu.make_async_copy(proj_out, out_buf, small.at[1])
-    get_in = pltpu.make_async_copy(proj_in, in_buf, small.at[2])
     get_used.start()
-    get_out.start()
+    if not held:
+        get_out = pltpu.make_async_copy(proj_out, out_buf, small.at[1])
+        get_in = pltpu.make_async_copy(proj_in, in_buf, small.at[2])
+        get_out.start()
+        get_in.start()
     for copy in copies(0):
         copy.start()
-    get_in.start()
     get_used.wait()
 
     @pl.loop(1, blocks)
@@ -60,8 +64,9 @@
             for copy in copies(j):
                 copy.start()
 
-    get_out.wait()
-    get_in.wait()
+    if not held:
+        get_out.wait()
+        get_in.wait()
 
     @pl.loop(0, blocks)
     def _(j):
@@ -86,34 +91,37 @@
             out[j] = jnp.zeros((BLOCK, 2 * rank), jnp.float32)
 
 
-def project(peer, count, slot, *args):
+def project(peer, count, slot, *args, held=False):
     lengths, acts, grads, proj_in, proj_out = args
     blocks = count * slot // BLOCK
     width = proj_out.shape[0] + proj_in.shape[0]
     rows = blocks * BLOCK
     depth = acts.shape[1] + grads.shape[1]
+    outside = 3 if held else 5
+    args = [pltpu.with_memory_space_constraint(x, pltpu.HBM) for x in args[:outside]] + [
+        *args[outside:]
+    ]
+    out_shape = [jax.ShapeDtypeStruct((blocks, BLOCK, width), jnp.float32)]
+    if not held:
+        out_shape += [jax.ShapeDtypeStruct(x.shape, x.dtype) for x in (proj_in, proj_out)]
     return pl.pallas_call(
-        functools.partial(project_kernel, peer, count, slot),
-        out_shape=jax.ShapeDtypeStruct((blocks, BLOCK, width), jnp.float32),
-        in_specs=[HBM] * 5,
-        out_specs=VMEM,
+        functools.partial(project_kernel, peer, count, slot, held),
+        out_shape=out_shape,
+        in_specs=[HBM] * outside + [VMEM] * (5 - outside),
+        out_specs=[VMEM] * len(out_shape),
         scratch_shapes=[
             pltpu.SMEM(lengths.shape, jnp.int32),
             pltpu.VMEM((blocks, BLOCK, acts.shape[1]), acts.dtype),
             pltpu.VMEM((blocks, BLOCK, grads.shape[1]), grads.dtype),
-            pltpu.VMEM(proj_in.shape, proj_in.dtype),
-            pltpu.VMEM(proj_out.shape, proj_out.dtype),
             pltpu.SemaphoreType.DMA((2, blocks)),
             pltpu.SemaphoreType.DMA((3,)),
         ],
-        compiler_params=pltpu.CompilerParams(
-            vmem_limit_bytes=2 * (rows + width) * depth + (6 << 20)
-        ),
+        compiler_params=pltpu.CompilerParams(vmem_limit_bytes=2 * rows * depth + (6 << 20)),
         cost_estimate=pl.CostEstimate(
             flops=width * rows * depth, bytes_accessed=2 * rows * depth, transcendentals=0
         ),
         name="project",
-    )(*[pltpu.with_memory_space_constraint(x, pltpu.HBM) for x in args])
+    )(*args)
 
 
 def hi_lo(x):
@@ -225,15 +233,15 @@
             blocks[m] = swap(queries, m)
     if halves:
         count = ex_count // 2
-        theirs = project(True, count, slot, *args)
+        theirs, *factors = project(True, count, slot, *args)
         arrived = lax.ppermute(theirs, "tensor", [(0, 1), (1, 0)])
-        parts = [project(False, count, slot, *args), arrived]
+        parts = [project(False, count, slot, *args[:3], *factors, held=True)[0], arrived]
     else:
         count = ex_count
-        parts = [lax.psum(project(None, count, slot, *args), "tensor")]
-    early = {m: blocks[m] for m in blocks if m < 6}
-    early, parts = lax.optimization_barrier((early, parts))
-    blocks = {**blocks, **early}
+        parts = [lax.psum(project(None, count, slot, *args)[0], "tensor")]
+    early = [m for m in reversed(bits[:NEAR_BITS])]
+    held, parts[0] = lax.optimization_barrier(([blocks[m] for m in early], parts[0]))
+    blocks.update(zip(early, held))
     own = units(parts, count, slot, rank_out, split, near, rest)
     if halves:
         own = jnp.concatenate([own, lax.ppermute(own, "tensor", [(0, 1), (1, 0)])], axis=1)

time: 39.4 us -> 38.7 us (0.982)
  starting transfers between devices: 19.2 us -> 13 us
  waiting for transfers between devices: 7.2 us -> 11.4 us
  Pallas kernels: 12.4 us -> 13.5 us
    ppermute x9, starting transfers between devices: 16.6 us -> 7.31 us  [swap(): return lax.ppermute(x, 'dp', xor_pairs(lax.axis_size('dp'), mask))]
    ppermute x1, starting transfers between devices: 0.73 us -> 5.66 us  [on_device(): arrived = lax.ppermute(theirs, 'tensor', [(0, 1), (1, 0)])]
    ppermute x9, waiting for transfers between devices: 5.07 us -> 7.46 us  [swap(): return lax.ppermute(x, 'dp', xor_pairs(lax.axis_size('dp'), mask))]
    ppermute x1, starting transfers between devices: 1.86 us -> 0.07 us  [on_device(): lax.ppermute(own, 'tensor', [(0, 1), (1, 0)])]
    ppermute x1, waiting for transfers between devices: 2.12 us -> 3.9 us  [on_device(): lax.ppermute(own, 'tensor', [(0, 1), (1, 0)])]
    pallas_call x2, Pallas kernels: 11.1 us -> 12.1 us  [project(): pl.pallas_call(functools.partial(project_kernel, peer, count, slot, held)...]
  transfers between devices with their start and end apart: 11 -> 11, of which waited for: 3 -> 3; matrix products, arithmetic and copies ran while one was open for 0% -> 0% of each run, Pallas kernels for 30% -> 33%
where the time goes in v1:
time: 38.7 us; the launch traced here: 38.6 us
  Pallas kernels  13.5 us (35%)
  starting transfers between devices  13 us (34%)
  waiting for transfers between devices  11.4 us (29%)
  other arithmetic  0.67 us (2%)
    pallas_call x2, Pallas kernels, project(): pl.pallas_call(functools.partial(project_kernel, peer, count, slot, held)...  12.1 us
    ppermute x9, waiting for transfers between devices, swap(): return lax.ppermute(x, 'dp', xor_pairs(lax.axis_size('dp'), mask))  7.46 us
    ppermute x9, starting transfers between devices, swap(): return lax.ppermute(x, 'dp', xor_pairs(lax.axis_size('dp'), mask))  7.31 us
    ppermute x1, starting transfers between devices, on_device(): arrived = lax.ppermute(theirs, 'tensor', [(0, 1), (1, 0)])  5.66 us
    ppermute x1, waiting for transfers between devices, on_device(): lax.ppermute(own, 'tensor', [(0, 1), (1, 0)])  3.9 us
  transfers between devices with their start and end apart: 11, of which 3 were waited for; matrix products, arithmetic and copies ran while one was open for 0% of the time, Pallas kernels for 33%

profile of v1, /device:TPU:0, one launch (start us, length us, event | category | flops | bytes accessed | tf_op | source)
XLA Modules:
  0.0 38.6 jit_solution(9218511592192412788)
XLA Ops:
  0.0 0.0 copy-start
  0.0 3.0 %collective-permute-start = (f32[256,256]{1,0:T(8,128)}, f32[256,256]{1,0:T(8,128)S(1)}, u32[]{:S(2)}, u32[]{:S(2)}) collective-permute-start(f32[256,256]{1,0:T(8,128)} %refs_2_), channel_id=1, source_target_pairs={{0,8},{2,10},{4,12},{6,14},{8,0},{10,2},{12,4},{14,6},{16,24},{18,... | collective-permute-start | bytes 786440 | tf_op jit(solution)/shard_map/ppermute | solution.py:23
  3.0 1.5 %collective-permute-start.1 = (f32[256,256]{1,0:T(8,128)}, f32[256,256]{1,0:T(8,128)S(1)}, u32[]{:S(2)}, u32[]{:S(2)}) collective-permute-start(f32[256,256]{1,0:T(8,128)} %refs_2_), channel_id=1, source_target_pairs={{0,4},{2,6},{4,0},{6,2},{8,12},{10,14},{12,8},{14,10},{16,20},{18,... | collective-permute-start | bytes 786440 | tf_op jit(solution)/shard_map/ppermute | solution.py:23
  4.5 0.0 collective-permute-start.2
  4.5 4.3 %project.2 = (f32[8,64,128]{2,1,0:T(8,128)S(1)}, bf16[64,4096]{1,0:T(8,128)(2,1)S(1)}, bf16[64,14336]{1,0:T(8,128)(2,1)S(1)}) custom-call(s32[4]{0:T(128)} %lengths.3, bf16[1024,4096]{1,0:T(8,128)(2,1)} %acts.3, bf16[1024,14336]{1,0:T(8,128)(2,1)} %grads.3, bf16[64,4096]{1,0:T(8,128)(2,1)} %refs_0_.1, bf16[64,14336]{1,0:T(8,128)(2,1)} %refs_1_.1), custom_call_target="tpu_custom_call" | custom-call | flops 1207959552 | bytes 18874368 | tf_op jit(solution)/shard_map/project/pallas_call | solution.py:107
  8.9 5.7 %collective-permute-start.3 = (f32[8,64,128]{2,1,0:T(8,128)S(1)}, f32[8,64,128]{2,1,0:T(8,128)S(1)}, u32[]{:S(2)}, u32[]{:S(2)}) collective-permute-start(f32[8,64,128]{2,1,0:T(8,128)S(1)} %get-tuple-element.23), channel_id=1, source_target_pairs={{0,1},{1,0},{2,3},{3,2},{4,5},{5,4},{6,7},{7,6},{8,9},{9,8},{10,11... | collective-permute-start | bytes 786440 | tf_op jit(solution)/shard_map/ppermute | solution.py:237
  14.5 0.0 copy-done
  14.5 0.0 collective-permute-start.5
  14.5 0.0 copy-start.1
  14.5 7.8 %project.3 = f32[8,64,128]{2,1,0:T(8,128)S(1)} custom-call(s32[4]{0:T(128)} %lengths.3, bf16[1024,4096]{1,0:T(8,128)(2,1)} %acts.3, bf16[1024,14336]{1,0:T(8,128)(2,1)} %grads.3, bf16[64,4096]{1,0:T(8,128)(2,1)S(1)} %get-tuple-element.20.refs_0_, bf16[64,14336]{1,0:T(8,128)(2,1)S(1)} %get-tuple-element.21.refs_1_), custom_call_target="tpu_custom_call" | custom-call | flops 1207959552 | bytes 18874368 | tf_op jit(solution)/shard_map/project/pallas_call | solution.py:107
  22.3 0.0 collective-permute-done.refs_6_
  22.4 0.0 collective-permute-done.1.refs_4_
  22.4 0.0 collective-permute-done.2.refs_3_
  22.4 0.0 collective-permute-done.3
  22.4 0.7 %units.1 = f32[2,2,8,256]{3,2,1,0:T(8,128)S(1)} custom-call(f32[2,256,128]{2,1,0:T(8,128)S(1)} %bitcast.6, f32[2,256,128]{2,1,0:T(8,128)S(1)} %bitcast.7), custom_call_target="tpu_custom_call" | custom-call | tf_op jit(solution)/shard_map/units/pallas_call | solution.py:161
  23.1 0.1 collective-permute-start.4
  23.2 3.9 %collective-permute-done.4 = f32[2,2,8,256]{3,2,1,0:T(8,128)S(1)} collective-permute-done((f32[2,2,8,256]{3,2,1,0:T(8,128)S(1)}, f32[2,2,8,256]{3,2,1,0:T(8,128)S(1)}, u32[]{:S(2)}, u32[]{:S(2)}) %collective-permute-start.4) | collective-permute-done | bytes 32800 | tf_op jit(solution)/shard_map/ppermute | solution.py:247
  27.1 0.0 collective-permute-done.5.refs_8_
  27.1 0.1 collective-permute-start.7
  27.2 0.5 %collective-permute-start.8 = (f32[256,256]{1,0:T(8,128)S(1)}, f32[256,256]{1,0:T(8,128)S(1)}, u32[]{:S(2)}, u32[]{:S(2)}) collective-permute-start(f32[256,256]{1,0:T(8,128)S(1)} %collective-permute-done.refs_6_), channel_id=1, source_target_pairs={{0,2},{2,0},{4,6},{6,4},{8,10},{10,8},{12,14},{14,12},{16,18},{18,... | collective-permute-start | bytes 786440 | tf_op jit(solution)/shard_map/ppermute | solution.py:23
  27.7 0.1 collective-permute-start.9
  27.7 1.1 %collective-permute-start.6 = (f32[4,8,256]{2,1,0:T(8,128)S(1)}, f32[4,8,256]{2,1,0:T(8,128)S(1)}, u32[]{:S(2)}, u32[]{:S(2)}) collective-permute-start(f32[4,8,256]{2,1,0:T(8,128)S(1)} %get-tuple-element.35), channel_id=1, source_target_pairs={{0,16},{2,18},{4,20},{6,22},{8,24},{10,26},{12,28},{14,30},{16,0},... | collective-permute-start | bytes 98312 | tf_op jit(solution)/shard_map/ppermute | solution.py:23
  28.9 3.9 %collective-permute-done.6.refs_1_ = f32[4,8,256]{2,1,0:T(8,128)S(1)} collective-permute-done((f32[4,8,256]{2,1,0:T(8,128)S(1)}, f32[4,8,256]{2,1,0:T(8,128)S(1)}, u32[]{:S(2)}, u32[]{:S(2)}) %collective-permute-start.6) | collective-permute-done | bytes 32800 | tf_op jit(solution)/shard_map/ppermute | solution.py:23
  32.7 0.0 collective-permute-done.7.refs_5_
  32.7 0.0 collective-permute-done.8.refs_7_
  32.7 0.0 collective-permute-done.9.refs_9_
  32.7 0.6 %scores.1 = (f32[4,256]{1,0:T(4,128)S(1)}, f32[4,256]{1,0:T(4,128)S(1)}) custom-call(f32[4,8,256]{2,1,0:T(8,128)S(1)} %get-tuple-element.36.refs_0_, f32[4,8,256]{2,1,0:T(8,128)S(1)} %collective-permute-done.6.refs_1_, f32[256,256]{1,0:T(8,128)S(1)} %copy-done, f32[256,256]{1,0:T(8,128)S(1)} %collective-permute-done.2.refs_3_, ...), custom_call_target="tpu_custom_call" | custom-call | tf_op jit(solution)/shard_map/scores/pallas_call | solution.py:203
  33.4 1.0 %collective-permute-start.10 = (f32[4,256]{1,0:T(4,128)S(1)}, f32[4,256]{1,0:T(4,128)S(1)}, u32[]{:S(2)}, u32[]{:S(2)}) collective-permute-start(f32[4,256]{1,0:T(4,128)S(1)} %get-tuple-element.34), channel_id=1, source_target_pairs={{0,16},{2,18},{4,20},{6,22},{8,24},{10,26},{12,28},{14,30},{16,0},... | collective-permute-start | bytes 12296 | tf_op jit(solution)/shard_map/ppermute | solution.py:23
  34.4 3.6 %collective-permute-done.10 = f32[4,256]{1,0:T(4,128)S(1)} collective-permute-done((f32[4,256]{1,0:T(4,128)S(1)}, f32[4,256]{1,0:T(4,128)S(1)}, u32[]{:S(2)}, u32[]{:S(2)}) %collective-permute-start.10) | collective-permute-done | bytes 4128 | tf_op jit(solution)/shard_map/ppermute | solution.py:23
  38.0 0.0 copy-done.1
  38.0 0.7 %add_select_fusion = f32[4,256]{1,0:T(4,128)} fusion(f32[4,256]{1,0:T(4,128)S(1)} %get-tuple-element.33, f32[4,256]{1,0:T(4,128)S(1)} %collective-permute-done.10, s32[256]{0:T(256)S(1)} %copy-done.1, s32[4]{0:T(128)S(1)} %iota_add_fusion), kind=kLoop, calls=%fused_computation.3 | loop fusion | flops 3072 | bytes 13328 | tf_op jit(solution)/shard_map/jit(_where)/select_n | solution.py:261
  (3 shorter events, 0.0 us)
Async XLA Ops:
  0.0 14.5 %copy-start = (f32[256,256]{1,0:T(8,128)S(1)}, f32[256,256]{1,0:T(8,128)}, u32[]{:S(2)}) copy-start(f32[256,256]{1,0:T(8,128)} %refs_2_) | copy-start | bytes 786436
  0.0 22.3 %collective-permute-start = (f32[256,256]{1,0:T(8,128)}, f32[256,256]{1,0:T(8,128)S(1)}, u32[]{:S(2)}, u32[]{:S(2)}) collective-permute-start(f32[256,256]{1,0:T(8,128)} %refs_2_), channel_id=1, source_target_pairs={{0,8},{2,10},{4,12},{6,14},{8,0},{10,2},{12,4},{14,6},{16,24},{18,... | collective-permute-start | bytes 786440 | tf_op jit(solution)/shard_map/ppermute | solution.py:23
  3.0 19.3 %collective-permute-start.1 = (f32[256,256]{1,0:T(8,128)}, f32[256,256]{1,0:T(8,128)S(1)}, u32[]{:S(2)}, u32[]{:S(2)}) collective-permute-start(f32[256,256]{1,0:T(8,128)} %refs_2_), channel_id=1, source_target_pairs={{0,4},{2,6},{4,0},{6,2},{8,12},{10,14},{12,8},{14,10},{16,20},{18,... | collective-permute-start | bytes 786440 | tf_op jit(solution)/shard_map/ppermute | solution.py:23
  4.5 17.8 %collective-permute-start.2 = (f32[256,256]{1,0:T(8,128)}, f32[256,256]{1,0:T(8,128)S(1)}, u32[]{:S(2)}, u32[]{:S(2)}) collective-permute-start(f32[256,256]{1,0:T(8,128)} %refs_2_), channel_id=1, source_target_pairs={{0,2},{2,0},{4,6},{6,4},{8,10},{10,8},{12,14},{14,12},{16,18},{18,... | collective-permute-start | bytes 786440 | tf_op jit(solution)/shard_map/ppermute | solution.py:23
  8.9 13.5 %collective-permute-start.3 = (f32[8,64,128]{2,1,0:T(8,128)S(1)}, f32[8,64,128]{2,1,0:T(8,128)S(1)}, u32[]{:S(2)}, u32[]{:S(2)}) collective-permute-start(f32[8,64,128]{2,1,0:T(8,128)S(1)} %get-tuple-element.23), channel_id=1, source_target_pairs={{0,1},{1,0},{2,3},{3,2},{4,5},{5,4},{6,7},{7,6},{8,9},{9,8},{10,11... | collective-permute-start | bytes 786440 | tf_op jit(solution)/shard_map/ppermute | solution.py:237
  14.5 12.6 %collective-permute-start.5 = (f32[256,256]{1,0:T(8,128)S(1)}, f32[256,256]{1,0:T(8,128)S(1)}, u32[]{:S(2)}, u32[]{:S(2)}) collective-permute-start(f32[256,256]{1,0:T(8,128)S(1)} %copy-done), channel_id=1, source_target_pairs={{0,12},{2,14},{4,8},{6,10},{8,4},{10,6},{12,0},{14,2},{16,28},{18,... | collective-permute-start | bytes 786440 | tf_op jit(solution)/shard_map/ppermute | solution.py:23
  14.5 23.5 %copy-start.1 = (s32[256]{0:T(256)S(1)}, s32[256]{0:T(256)}, u32[]{:S(2)}) copy-start(s32[256]{0:T(256)} %param.13) | copy-start | bytes 3076
  23.1 4.0 %collective-permute-start.4 = (f32[2,2,8,256]{3,2,1,0:T(8,128)S(1)}, f32[2,2,8,256]{3,2,1,0:T(8,128)S(1)}, u32[]{:S(2)}, u32[]{:S(2)}) collective-permute-start(f32[2,2,8,256]{3,2,1,0:T(8,128)S(1)} %units.1), channel_id=1, source_target_pairs={{0,1},{1,0},{2,3},{3,2},{4,5},{5,4},{6,7},{7,6},{8,9},{9,8},{10,11... | collective-permute-start | bytes 98312 | tf_op jit(solution)/shard_map/ppermute | solution.py:247
  27.1 5.7 %collective-permute-start.7 = (f32[256,256]{1,0:T(8,128)S(1)}, f32[256,256]{1,0:T(8,128)S(1)}, u32[]{:S(2)}, u32[]{:S(2)}) collective-permute-start(f32[256,256]{1,0:T(8,128)S(1)} %collective-permute-done.1.refs_4_), channel_id=1, source_target_pairs={{0,2},{2,0},{4,6},{6,4},{8,10},{10,8},{12,14},{14,12},{16,18},{18,... | collective-permute-start | bytes 786440 | tf_op jit(solution)/shard_map/ppermute | solution.py:23
  27.2 5.6 %collective-permute-start.8 = (f32[256,256]{1,0:T(8,128)S(1)}, f32[256,256]{1,0:T(8,128)S(1)}, u32[]{:S(2)}, u32[]{:S(2)}) collective-permute-start(f32[256,256]{1,0:T(8,128)S(1)} %collective-permute-done.refs_6_), channel_id=1, source_target_pairs={{0,2},{2,0},{4,6},{6,4},{8,10},{10,8},{12,14},{14,12},{16,18},{18,... | collective-permute-start | bytes 786440 | tf_op jit(solution)/shard_map/ppermute | solution.py:23
  27.7 5.1 %collective-permute-start.9 = (f32[256,256]{1,0:T(8,128)S(1)}, f32[256,256]{1,0:T(8,128)S(1)}, u32[]{:S(2)}, u32[]{:S(2)}) collective-permute-start(f32[256,256]{1,0:T(8,128)S(1)} %collective-permute-done.5.refs_8_), channel_id=1, source_target_pairs={{0,2},{2,0},{4,6},{6,4},{8,10},{10,8},{12,14},{14,12},{16,18},{18,... | collective-permute-start | bytes 786440 | tf_op jit(solution)/shard_map/ppermute | solution.py:23
  27.7 5.0 %collective-permute-start.6 = (f32[4,8,256]{2,1,0:T(8,128)S(1)}, f32[4,8,256]{2,1,0:T(8,128)S(1)}, u32[]{:S(2)}, u32[]{:S(2)}) collective-permute-start(f32[4,8,256]{2,1,0:T(8,128)S(1)} %get-tuple-element.35), channel_id=1, source_target_pairs={{0,16},{2,18},{4,20},{6,22},{8,24},{10,26},{12,28},{14,30},{16,0},... | collective-permute-start | bytes 98312 | tf_op jit(solution)/shard_map/ppermute | solution.py:23
  33.4 4.6 %collective-permute-start.10 = (f32[4,256]{1,0:T(4,128)S(1)}, f32[4,256]{1,0:T(4,128)S(1)}, u32[]{:S(2)}, u32[]{:S(2)}) collective-permute-start(f32[4,256]{1,0:T(4,128)S(1)} %get-tuple-element.34), channel_id=1, source_target_pairs={{0,16},{2,18},{4,20},{6,22},{8,24},{10,26},{12,28},{14,30},{16,0},... | collective-permute-start | bytes 12296 | tf_op jit(solution)/shard_map/ppermute | solution.py:23

commit v2 on v1

--- a/solution.py
+++ b/solution.py
@@ -8,6 +8,7 @@
 from jax.sharding import PartitionSpec as P
 
 BLOCK = 64
+WINDOW = 5
 NEAR_BITS = 3
 NT = (((1,), (1,)), ((), ()))
 TN = (((0,), (0,)), ((), ()))
@@ -25,15 +26,20 @@
 
 def project_kernel(peer, count, slot, held, lengths, acts, grads, *refs):
     if held:
-        in_buf, out_buf, out, used, act_buf, grad_buf, sems, small = refs
+        in_buf, out_buf, _, _, out, act_buf, grad_buf, sems, small = refs
+        used = lengths
+    elif peer:
+        proj_in, proj_out, out, in_buf, out_buf, next_act, next_grad = refs[:7]
+        used, act_buf, grad_buf, sems, small = refs[7:]
     else:
-        proj_in, proj_out, out, in_buf, out_buf, used, act_buf, grad_buf, sems, small = refs
+        proj_in, proj_out, out, used, in_buf, out_buf, act_buf, grad_buf, sems, small = refs
     per = slot // BLOCK
     blocks = count * per
-    first = 0
+    first = other = 0
     if peer is not None:
         mine = lax.axis_index("tensor")
         first = (1 - mine if peer else mine) * count
+        other = count - first
     rank = out_buf.shape[0]
 
     def copies(j):
@@ -46,36 +52,76 @@
     def left(j):
         return used[first + j // per] - (j % per) * BLOCK
 
-    get_used = pltpu.make_async_copy(lengths, used, small.at[0])
-    get_used.start()
+    if not held:
+        get_used = pltpu.make_async_copy(lengths, used, small.at[0])
+        get_used.start()
+    ahead = []
     if not held:
         get_out = pltpu.make_async_copy(proj_out, out_buf, small.at[1])
         get_in = pltpu.make_async_copy(proj_in, in_buf, small.at[2])
         get_out.start()
         get_in.start()
-    for copy in copies(0):
-        copy.start()
-    get_used.wait()
-
-    @pl.loop(1, blocks)
-    def _(j):
-        @pl.when(left(j) > 0)
+        for copy in copies(0):
+            copy.start()
+    if peer:
+        for e in range(count):
+            row = pl.multiple_of((other + e) * slot, BLOCK)
+            for data, buf in ((grads, next_grad), (acts, next_act)):
+                ahead.append(
+                    pltpu.make_async_copy(
+                        data.at[pl.ds(row, BLOCK)], buf.at[e * per], small.at[3 + len(ahead)]
+                    )
+                )
+    if not held:
+        get_used.wait()
+
+    def place(i):
+        if not held:
+            return i
+        rest = i - count
+        later = rest // (per - 1) * per + rest % (per - 1) + 1
+        return jnp.where(i < count, i * per, later)
+
+    def fetch(i):
+        j = place(jnp.minimum(i, blocks - 1))
+
+        @pl.when((i < blocks) & (left(j) > 0))
         def _():
             for copy in copies(j):
                 copy.start()
 
+    @pl.loop(count if held else 1, WINDOW if held else blocks)
+    def _(i):
+        fetch(i)
+
     if not held:
         get_out.wait()
         get_in.wait()
 
     @pl.loop(0, blocks)
-    def _(j):
+    def _(i):
+        j = place(i)
         rows = left(j)
+        if held:
+            fetch(i + WINDOW)
+        if peer:
+
+            @pl.when(i == 2)
+            def _():
+                for copy in ahead:
+                    copy.start()
 
         @pl.when(rows > 0)
         def _():
-            for copy in copies(j):
-                copy.wait()
+            if held:
+
+                @pl.when(i >= count)
+                def _():
+                    for copy in copies(j):
+                        copy.wait()
+            else:
+                for copy in copies(j):
+                    copy.wait()
             part_grads = lax.dot_general(
                 grad_buf[j], out_buf[...], NT, preferred_element_type=jnp.float32
             )
@@ -90,38 +136,52 @@
         def _():
             out[j] = jnp.zeros((BLOCK, 2 * rank), jnp.float32)
 
-
-def project(peer, count, slot, *args, held=False):
-    lengths, acts, grads, proj_in, proj_out = args
+    for copy in ahead:
+        copy.wait()
+
+
+def project(peer, count, slot, *args, held=()):
+    lengths, acts, grads = args[:3]
     blocks = count * slot // BLOCK
-    width = proj_out.shape[0] + proj_in.shape[0]
+    factors = held[:2] if held else args[3:]
+    width = factors[0].shape[0] + factors[1].shape[0]
     rows = blocks * BLOCK
     depth = acts.shape[1] + grads.shape[1]
-    outside = 3 if held else 5
-    args = [pltpu.with_memory_space_constraint(x, pltpu.HBM) for x in args[:outside]] + [
-        *args[outside:]
+    outside = args[:3] if held else args
+    operands = [pltpu.with_memory_space_constraint(x, pltpu.HBM) for x in outside] + [*held]
+    in_specs = [HBM] * len(outside) + [VMEM] * len(held)
+    if held:
+        operands[0], in_specs[0] = lengths, pl.BlockSpec(memory_space=pltpu.SMEM)
+    bufs = [(blocks, BLOCK, acts.shape[1]), (blocks, BLOCK, grads.shape[1])]
+    out_shape = [jax.ShapeDtypeStruct((blocks, BLOCK, width), jnp.float32)]
+    scratch_shapes = [] if held else [pltpu.SMEM(lengths.shape, jnp.int32)]
+    if peer:
+        out_shape += [jax.ShapeDtypeStruct(x.shape, x.dtype) for x in factors]
+    elif not held:
+        scratch_shapes += [pltpu.VMEM(x.shape, x.dtype) for x in factors]
+    if peer is None or peer:
+        scratch_shapes += [pltpu.VMEM(shape, acts.dtype) for shape in bufs]
+    if peer is not None:
+        out_shape += [jax.ShapeDtypeStruct(shape, acts.dtype) for shape in bufs]
+    scratch_shapes += [
+        pltpu.SemaphoreType.DMA((2, blocks)),
+        pltpu.SemaphoreType.DMA((3 + 2 * count,)),
     ]
-    out_shape = [jax.ShapeDtypeStruct((blocks, BLOCK, width), jnp.float32)]
-    if not held:
-        out_shape += [jax.ShapeDtypeStruct(x.shape, x.dtype) for x in (proj_in, proj_out)]
     return pl.pallas_call(
-        functools.partial(project_kernel, peer, count, slot, held),
+        functools.partial(project_kernel, peer, count, slot, bool(held)),
         out_shape=out_shape,
-        in_specs=[HBM] * outside + [VMEM] * (5 - outside),
+        in_specs=in_specs,
         out_specs=[VMEM] * len(out_shape),
-        scratch_shapes=[
-            pltpu.SMEM(lengths.shape, jnp.int32),
-            pltpu.VMEM((blocks, BLOCK, acts.shape[1]), acts.dtype),
-            pltpu.VMEM((blocks, BLOCK, grads.shape[1]), grads.dtype),
-            pltpu.SemaphoreType.DMA((2, blocks)),
-            pltpu.SemaphoreType.DMA((3,)),
-        ],
-        compiler_params=pltpu.CompilerParams(vmem_limit_bytes=2 * rows * depth + (6 << 20)),
+        scratch_shapes=scratch_shapes,
+        input_output_aliases={5: 1, 6: 2} if held else {},
+        compiler_params=pltpu.CompilerParams(
+            vmem_limit_bytes=(6 << 20) if held else 2 * (rows + width) * depth + (4 << 20)
+        ),
         cost_estimate=pl.CostEstimate(
             flops=width * rows * depth, bytes_accessed=2 * rows * depth, transcendentals=0
         ),
         name="project",
-    )(*args)
+    )(*operands)
 
 
 def hi_lo(x):
@@ -233,9 +293,9 @@
             blocks[m] = swap(queries, m)
     if halves:
         count = ex_count // 2
-        theirs, *factors = project(True, count, slot, *args)
+        theirs, *held = project(True, count, slot, *args)
         arrived = lax.ppermute(theirs, "tensor", [(0, 1), (1, 0)])
-        parts = [project(False, count, slot, *args[:3], *factors, held=True)[0], arrived]
+        parts = [project(False, count, slot, *args[:3], held=held)[0], arrived]
     else:
         count = ex_count
         parts = [lax.psum(project(None, count, slot, *args)[0], "tensor")]

time: 38.7 us -> 38.3 us (0.990)
  starting transfers between devices: 13 us -> 11.2 us
  Pallas kernels: 13.5 us -> 14.9 us
  waiting for transfers between devices: 11.4 us -> 11 us
    ppermute x1, starting transfers between devices: 5.66 us -> 3.39 us  [on_device(): arrived = lax.ppermute(theirs, 'tensor', [(0, 1), (1, 0)])]
    pallas_call x2, Pallas kernels: 12.1 us -> 13.6 us  [project(): pl.pallas_call(functools.partial(project_kernel, peer, count, slot, bool(...]
    ppermute x9, starting transfers between devices: 7.31 us -> 7.7 us  [swap(): return lax.ppermute(x, 'dp', xor_pairs(lax.axis_size('dp'), mask))]
  transfers between devices with their start and end apart: 11 -> 11, of which waited for: 3 -> 3; matrix products, arithmetic and copies ran while one was open for 0% -> 0% of each run, Pallas kernels for 33% -> 38%
where the time goes in v2:
time: 38.3 us; the launch traced here: 37.9 us
  Pallas kernels  14.9 us (39%)
  starting transfers between devices  11.2 us (29%)
  waiting for transfers between devices  11 us (29%)
  other arithmetic  0.67 us (2%)
    pallas_call x2, Pallas kernels, project(): pl.pallas_call(functools.partial(project_kernel, peer, count, slot, bool(...  13.6 us
    ppermute x9, starting transfers between devices, swap(): return lax.ppermute(x, 'dp', xor_pairs(lax.axis_size('dp'), mask))  7.7 us
    ppermute x9, waiting for transfers between devices, swap(): return lax.ppermute(x, 'dp', xor_pairs(lax.axis_size('dp'), mask))  7.1 us
    ppermute x1, waiting for transfers between devices, on_device(): lax.ppermute(own, 'tensor', [(0, 1), (1, 0)])  3.87 us
    ppermute x1, starting transfers between devices, on_device(): arrived = lax.ppermute(theirs, 'tensor', [(0, 1), (1, 0)])  3.39 us
  transfers between devices with their start and end apart: 11, of which 3 were waited for; matrix products, arithmetic and copies ran while one was open for 0% of the time, Pallas kernels for 38%

profile of v2, /device:TPU:0, one launch (start us, length us, event | category | flops | bytes accessed | tf_op | source)
XLA Modules:
  0.0 37.9 jit_solution(5210892552773466606)
XLA Ops:
  0.0 0.0 copy-start
  0.0 0.0 copy-start.1
  0.0 3.0 %collective-permute-start = (f32[256,256]{1,0:T(8,128)}, f32[256,256]{1,0:T(8,128)S(1)}, u32[]{:S(2)}, u32[]{:S(2)}) collective-permute-start(f32[256,256]{1,0:T(8,128)} %refs_2_), channel_id=1, source_target_pairs={{0,8},{2,10},{4,12},{6,14},{8,0},{10,2},{12,4},{14,6},{16,24},{18,... | collective-permute-start | bytes 786440 | tf_op jit(solution)/shard_map/ppermute | solution.py:24
  3.0 1.5 %collective-permute-start.1 = (f32[256,256]{1,0:T(8,128)}, f32[256,256]{1,0:T(8,128)S(1)}, u32[]{:S(2)}, u32[]{:S(2)}) collective-permute-start(f32[256,256]{1,0:T(8,128)} %refs_2_), channel_id=1, source_target_pairs={{0,4},{2,6},{4,0},{6,2},{8,12},{10,14},{12,8},{14,10},{16,20},{18,... | collective-permute-start | bytes 786440 | tf_op jit(solution)/shard_map/ppermute | solution.py:24
  4.5 0.0 collective-permute-start.2
  4.6 6.6 %project.2 = (f32[8,64,128]{2,1,0:T(8,128)S(1)}, bf16[64,4096]{1,0:T(8,128)(2,1)S(1)}, bf16[64,14336]{1,0:T(8,128)(2,1)S(1)}, bf16[8,64,4096]{2,1,0:T(8,128)(2,1)S(1)}, bf16[8,64,14336]{2,1,0:T(8,128)(2,1)S(1)}) custom-call(s32[4]{0:T(128)} %lengths.3, bf16[1024,4096]{1,0:T(8,128)(2,1)} %acts.3, bf16[1024,14336]{1,0:T(8,128)(2,1)} %grads.3, ...), custom_call_target="tpu_custom_call" | custom-call | flops 1207959552 | bytes 18874368 | tf_op jit(solution)/shard_map/project/pallas_call | solution.py:170
  11.2 3.4 %collective-permute-start.3 = (f32[8,64,128]{2,1,0:T(8,128)S(1)}, f32[8,64,128]{2,1,0:T(8,128)S(1)}, u32[]{:S(2)}, u32[]{:S(2)}) collective-permute-start(f32[8,64,128]{2,1,0:T(8,128)S(1)} %get-tuple-element.29), channel_id=1, source_target_pairs={{0,1},{1,0},{2,3},{3,2},{4,5},{5,4},{6,7},{7,6},{8,9},{9,8},{10,11... | collective-permute-start | bytes 786440 | tf_op jit(solution)/shard_map/ppermute | solution.py:297
  14.6 0.0 copy-done
  14.6 0.0 collective-permute-start.5
  14.6 0.0 copy-done.1
  14.6 0.0 copy-start.2
  14.6 7.0 %project.3 = (f32[8,64,128]{2,1,0:T(8,128)S(1)}, bf16[8,64,4096]{2,1,0:T(8,128)(2,1)S(1)}, bf16[8,64,14336]{2,1,0:T(8,128)(2,1)S(1)}) custom-call(s32[4]{0:T(128)S(1)} %copy-done.1, bf16[1024,4096]{1,0:T(8,128)(2,1)} %acts.3, bf16[1024,14336]{1,0:T(8,128)(2,1)} %grads.3, ...), custom_call_target="tpu_custom_call", output_to_operand_aliasing={{1}: (5, {}), {2}: (6, {})} | custom-call | flops 1207959552 | bytes 18874368 | tf_op jit(solution)/shard_map/project/pallas_call | solution.py:170
  21.6 0.0 collective-permute-done.refs_6_
  21.6 0.0 collective-permute-done.1.refs_4_
  21.6 0.0 collective-permute-done.2.refs_3_
  21.6 0.0 collective-permute-done.3
  21.6 0.7 %units.1 = f32[2,2,8,256]{3,2,1,0:T(8,128)S(1)} custom-call(f32[2,256,128]{2,1,0:T(8,128)S(1)} %bitcast.7, f32[2,256,128]{2,1,0:T(8,128)S(1)} %bitcast.6), custom_call_target="tpu_custom_call" | custom-call | tf_op jit(solution)/shard_map/units/pallas_call | solution.py:221
  22.3 0.1 collective-permute-start.4
  22.4 3.9 %collective-permute-done.4 = f32[2,2,8,256]{3,2,1,0:T(8,128)S(1)} collective-permute-done((f32[2,2,8,256]{3,2,1,0:T(8,128)S(1)}, f32[2,2,8,256]{3,2,1,0:T(8,128)S(1)}, u32[]{:S(2)}, u32[]{:S(2)}) %collective-permute-start.4) | collective-permute-done | bytes 32800 | tf_op jit(solution)/shard_map/ppermute | solution.py:307
  26.3 0.0 collective-permute-done.5.refs_8_
  26.3 0.1 collective-permute-start.7
  26.4 0.5 %collective-permute-start.8 = (f32[256,256]{1,0:T(8,128)S(1)}, f32[256,256]{1,0:T(8,128)S(1)}, u32[]{:S(2)}, u32[]{:S(2)}) collective-permute-start(f32[256,256]{1,0:T(8,128)S(1)} %collective-permute-done.refs_6_), channel_id=1, source_target_pairs={{0,2},{2,0},{4,6},{6,4},{8,10},{10,8},{12,14},{14,12},{16,18},{18,... | collective-permute-start | bytes 786440 | tf_op jit(solution)/shard_map/ppermute | solution.py:24
  26.9 0.1 collective-permute-start.9
  27.0 1.3 %collective-permute-start.6 = (f32[4,8,256]{2,1,0:T(8,128)S(1)}, f32[4,8,256]{2,1,0:T(8,128)S(1)}, u32[]{:S(2)}, u32[]{:S(2)}) collective-permute-start(f32[4,8,256]{2,1,0:T(8,128)S(1)} %get-tuple-element.41), channel_id=1, source_target_pairs={{0,16},{2,18},{4,20},{6,22},{8,24},{10,26},{12,28},{14,30},{16,0},... | collective-permute-start | bytes 98312 | tf_op jit(solution)/shard_map/ppermute | solution.py:24
  28.3 3.7 %collective-permute-done.6.refs_1_ = f32[4,8,256]{2,1,0:T(8,128)S(1)} collective-permute-done((f32[4,8,256]{2,1,0:T(8,128)S(1)}, f32[4,8,256]{2,1,0:T(8,128)S(1)}, u32[]{:S(2)}, u32[]{:S(2)}) %collective-permute-start.6) | collective-permute-done | bytes 32800 | tf_op jit(solution)/shard_map/ppermute | solution.py:24
  32.0 0.0 collective-permute-done.7.refs_5_
  32.0 0.0 collective-permute-done.8.refs_7_
  32.0 0.0 collective-permute-done.9.refs_9_
  32.0 0.6 %scores.1 = (f32[4,256]{1,0:T(4,128)S(1)}, f32[4,256]{1,0:T(4,128)S(1)}) custom-call(f32[4,8,256]{2,1,0:T(8,128)S(1)} %get-tuple-element.42.refs_0_, f32[4,8,256]{2,1,0:T(8,128)S(1)} %collective-permute-done.6.refs_1_, f32[256,256]{1,0:T(8,128)S(1)} %copy-done, f32[256,256]{1,0:T(8,128)S(1)} %collective-permute-done.2.refs_3_, ...), custom_call_target="tpu_custom_call" | custom-call | tf_op jit(solution)/shard_map/scores/pallas_call | solution.py:263
  32.7 1.2 %collective-permute-start.10 = (f32[4,256]{1,0:T(4,128)S(1)}, f32[4,256]{1,0:T(4,128)S(1)}, u32[]{:S(2)}, u32[]{:S(2)}) collective-permute-start(f32[4,256]{1,0:T(4,128)S(1)} %get-tuple-element.40), channel_id=1, source_target_pairs={{0,16},{2,18},{4,20},{6,22},{8,24},{10,26},{12,28},{14,30},{16,0},... | collective-permute-start | bytes 12296 | tf_op jit(solution)/shard_map/ppermute | solution.py:24
  33.8 3.4 %collective-permute-done.10 = f32[4,256]{1,0:T(4,128)S(1)} collective-permute-done((f32[4,256]{1,0:T(4,128)S(1)}, f32[4,256]{1,0:T(4,128)S(1)}, u32[]{:S(2)}, u32[]{:S(2)}) %collective-permute-start.10) | collective-permute-done | bytes 4128 | tf_op jit(solution)/shard_map/ppermute | solution.py:24
  37.2 0.0 copy-done.2
  37.2 0.7 %add_select_fusion = f32[4,256]{1,0:T(4,128)} fusion(f32[4,256]{1,0:T(4,128)S(1)} %get-tuple-element.39, f32[4,256]{1,0:T(4,128)S(1)} %collective-permute-done.10, s32[256]{0:T(256)S(1)} %copy-done.2, s32[4]{0:T(128)S(1)} %iota_add_fusion), kind=kLoop, calls=%fused_computation.3 | loop fusion | flops 3072 | bytes 13328 | tf_op jit(solution)/shard_map/jit(_where)/select_n | solution.py:321
  (3 shorter events, 0.0 us)
Async XLA Ops:
  0.0 14.6 %copy-start = (f32[256,256]{1,0:T(8,128)S(1)}, f32[256,256]{1,0:T(8,128)}, u32[]{:S(2)}) copy-start(f32[256,256]{1,0:T(8,128)} %refs_2_) | copy-start | bytes 786436
  0.0 14.6 %copy-start.1 = (s32[4]{0:T(128)S(1)}, s32[4]{0:T(128)}, u32[]{:S(2)}) copy-start(s32[4]{0:T(128)} %lengths.3) | copy-start | bytes 52
  0.0 21.6 %collective-permute-start = (f32[256,256]{1,0:T(8,128)}, f32[256,256]{1,0:T(8,128)S(1)}, u32[]{:S(2)}, u32[]{:S(2)}) collective-permute-start(f32[256,256]{1,0:T(8,128)} %refs_2_), channel_id=1, source_target_pairs={{0,8},{2,10},{4,12},{6,14},{8,0},{10,2},{12,4},{14,6},{16,24},{18,... | collective-permute-start | bytes 786440 | tf_op jit(solution)/shard_map/ppermute | solution.py:24
  3.0 18.5 %collective-permute-start.1 = (f32[256,256]{1,0:T(8,128)}, f32[256,256]{1,0:T(8,128)S(1)}, u32[]{:S(2)}, u32[]{:S(2)}) collective-permute-start(f32[256,256]{1,0:T(8,128)} %refs_2_), channel_id=1, source_target_pairs={{0,4},{2,6},{4,0},{6,2},{8,12},{10,14},{12,8},{14,10},{16,20},{18,... | collective-permute-start | bytes 786440 | tf_op jit(solution)/shard_map/ppermute | solution.py:24
  4.5 17.0 %collective-permute-start.2 = (f32[256,256]{1,0:T(8,128)}, f32[256,256]{1,0:T(8,128)S(1)}, u32[]{:S(2)}, u32[]{:S(2)}) collective-permute-start(f32[256,256]{1,0:T(8,128)} %refs_2_), channel_id=1, source_target_pairs={{0,2},{2,0},{4,6},{6,4},{8,10},{10,8},{12,14},{14,12},{16,18},{18,... | collective-permute-start | bytes 786440 | tf_op jit(solution)/shard_map/ppermute | solution.py:24
  11.2 10.4 %collective-permute-start.3 = (f32[8,64,128]{2,1,0:T(8,128)S(1)}, f32[8,64,128]{2,1,0:T(8,128)S(1)}, u32[]{:S(2)}, u32[]{:S(2)}) collective-permute-start(f32[8,64,128]{2,1,0:T(8,128)S(1)} %get-tuple-element.29), channel_id=1, source_target_pairs={{0,1},{1,0},{2,3},{3,2},{4,5},{5,4},{6,7},{7,6},{8,9},{9,8},{10,11... | collective-permute-start | bytes 786440 | tf_op jit(solution)/shard_map/ppermute | solution.py:297
  14.6 11.7 %collective-permute-start.5 = (f32[256,256]{1,0:T(8,128)S(1)}, f32[256,256]{1,0:T(8,128)S(1)}, u32[]{:S(2)}, u32[]{:S(2)}) collective-permute-start(f32[256,256]{1,0:T(8,128)S(1)} %copy-done), channel_id=1, source_target_pairs={{0,12},{2,14},{4,8},{6,10},{8,4},{10,6},{12,0},{14,2},{16,28},{18,... | collective-permute-start | bytes 786440 | tf_op jit(solution)/shard_map/ppermute | solution.py:24
  14.6 22.7 %copy-start.2 = (s32[256]{0:T(256)S(1)}, s32[256]{0:T(256)}, u32[]{:S(2)}) copy-start(s32[256]{0:T(256)} %param.13) | copy-start | bytes 3076
  22.3 4.0 %collective-permute-start.4 = (f32[2,2,8,256]{3,2,1,0:T(8,128)S(1)}, f32[2,2,8,256]{3,2,1,0:T(8,128)S(1)}, u32[]{:S(2)}, u32[]{:S(2)}) collective-permute-start(f32[2,2,8,256]{3,2,1,0:T(8,128)S(1)} %units.1), channel_id=1, source_target_pairs={{0,1},{1,0},{2,3},{3,2},{4,5},{5,4},{6,7},{7,6},{8,9},{9,8},{10,11... | collective-permute-start | bytes 98312 | tf_op jit(solution)/shard_map/ppermute | solution.py:307
  26.3 5.7 %collective-permute-start.7 = (f32[256,256]{1,0:T(8,128)S(1)}, f32[256,256]{1,0:T(8,128)S(1)}, u32[]{:S(2)}, u32[]{:S(2)}) collective-permute-start(f32[256,256]{1,0:T(8,128)S(1)} %collective-permute-done.1.refs_4_), channel_id=1, source_target_pairs={{0,2},{2,0},{4,6},{6,4},{8,10},{10,8},{12,14},{14,12},{16,18},{18,... | collective-permute-start | bytes 786440 | tf_op jit(solution)/shard_map/ppermute | solution.py:24
  26.4 5.6 %collective-permute-start.8 = (f32[256,256]{1,0:T(8,128)S(1)}, f32[256,256]{1,0:T(8,128)S(1)}, u32[]{:S(2)}, u32[]{:S(2)}) collective-permute-start(f32[256,256]{1,0:T(8,128)S(1)} %collective-permute-done.refs_6_), channel_id=1, source_target_pairs={{0,2},{2,0},{4,6},{6,4},{8,10},{10,8},{12,14},{14,12},{16,18},{18,... | collective-permute-start | bytes 786440 | tf_op jit(solution)/shard_map/ppermute | solution.py:24
  26.9 5.1 %collective-permute-start.9 = (f32[256,256]{1,0:T(8,128)S(1)}, f32[256,256]{1,0:T(8,128)S(1)}, u32[]{:S(2)}, u32[]{:S(2)}) collective-permute-start(f32[256,256]{1,0:T(8,128)S(1)} %collective-permute-done.5.refs_8_), channel_id=1, source_target_pairs={{0,2},{2,0},{4,6},{6,4},{8,10},{10,8},{12,14},{14,12},{16,18},{18,... | collective-permute-start | bytes 786440 | tf_op jit(solution)/shard_map/ppermute | solution.py:24
  27.0 5.0 %collective-permute-start.6 = (f32[4,8,256]{2,1,0:T(8,128)S(1)}, f32[4,8,256]{2,1,0:T(8,128)S(1)}, u32[]{:S(2)}, u32[]{:S(2)}) collective-permute-start(f32[4,8,256]{2,1,0:T(8,128)S(1)} %get-tuple-element.41), channel_id=1, source_target_pairs={{0,16},{2,18},{4,20},{6,22},{8,24},{10,26},{12,28},{14,30},{16,0},... | collective-permute-start | bytes 98312 | tf_op jit(solution)/shard_map/ppermute | solution.py:24
  32.7 4.6 %collective-permute-start.10 = (f32[4,256]{1,0:T(4,128)S(1)}, f32[4,256]{1,0:T(4,128)S(1)}, u32[]{:S(2)}, u32[]{:S(2)}) collective-permute-start(f32[4,256]{1,0:T(4,128)S(1)} %get-tuple-element.40), channel_id=1, source_target_pairs={{0,16},{2,18},{4,20},{6,22},{8,24},{10,26},{12,28},{14,30},{16,0},... | collective-permute-start | bytes 12296 | tf_op jit(solution)/shard_map/ppermute | solution.py:24

commit v3 on v2

--- a/solution.py
+++ b/solution.py
@@ -303,9 +303,12 @@
     held, parts[0] = lax.optimization_barrier(([blocks[m] for m in early], parts[0]))
     blocks.update(zip(early, held))
     own = units(parts, count, slot, rank_out, split, near, rest)
+    own, held = lax.optimization_barrier((own, [blocks[m] for m in bits[1:NEAR_BITS]]))
+    blocks.update(zip(bits[1:NEAR_BITS], held))
+    last = near[-1] ^ 1
     if halves:
         own = jnp.concatenate([own, lax.ppermute(own, "tensor", [(0, 1), (1, 0)])], axis=1)
-        own, blocks = lax.optimization_barrier((own, blocks))
+        own, blocks[last] = lax.optimization_barrier((own, blocks[last]))
     rows_of = [own[g] if r == 0 else swap(own[g], r) for g, r in enumerate(rest)]
     for m in near:
         if m > 1 and m % 2 == 1:

time: 38.3 us -> 37.5 us (0.979)
  waiting for transfers between devices: 11 us -> 5.97 us
  starting transfers between devices: 11.2 us -> 15.9 us
  Pallas kernels: 14.9 us -> 14.3 us
    ppermute x9, starting transfers between devices: 7.7 us -> 12.1 us  [swap(): return lax.ppermute(x, 'dp', xor_pairs(lax.axis_size('dp'), mask))]
    ppermute x9, waiting for transfers between devices: 7.1 us -> 3.66 us  [swap(): return lax.ppermute(x, 'dp', xor_pairs(lax.axis_size('dp'), mask))]
    ppermute x1, waiting for transfers between devices: 3.87 us -> 2.12 us  [on_device(): lax.ppermute(own, 'tensor', [(0, 1), (1, 0)])]
    ppermute x1, starting transfers between devices: 0.11 us -> 1.35 us  [on_device(): lax.ppermute(own, 'tensor', [(0, 1), (1, 0)])]
    ppermute x1, starting transfers between devices: 3.39 us -> 2.38 us  [on_device(): arrived = lax.ppermute(theirs, 'tensor', [(0, 1), (1, 0)])]
    pallas_call x2, Pallas kernels: 13.6 us -> 13 us  [project(): pl.pallas_call(functools.partial(project_kernel, peer, count, slot, bool(...]
  transfers between devices with their start and end apart: 11 -> 11, of which waited for: 3 -> 4; matrix products, arithmetic and copies ran while one was open for 0% -> 0% of each run, Pallas kernels for 38% -> 37%
where the time goes in v3:
time: 37.5 us; the launch traced here: 36.9 us
  starting transfers between devices  15.9 us (42%)
  Pallas kernels  14.3 us (38%)
  waiting for transfers between devices  5.97 us (16%)
  other arithmetic  0.67 us (2%)
    pallas_call x2, Pallas kernels, project(): pl.pallas_call(functools.partial(project_kernel, peer, count, slot, bool(...  13 us
    ppermute x9, starting transfers between devices, swap(): return lax.ppermute(x, 'dp', xor_pairs(lax.axis_size('dp'), mask))  12.1 us
    ppermute x9, waiting for transfers between devices, swap(): return lax.ppermute(x, 'dp', xor_pairs(lax.axis_size('dp'), mask))  3.66 us
    ppermute x1, starting transfers between devices, on_device(): arrived = lax.ppermute(theirs, 'tensor', [(0, 1), (1, 0)])  2.38 us
    ppermute x1, waiting for transfers between devices, on_device(): lax.ppermute(own, 'tensor', [(0, 1), (1, 0)])  2.12 us
    ppermute x1, starting transfers between devices, on_device(): lax.ppermute(own, 'tensor', [(0, 1), (1, 0)])  1.35 us
  transfers between devices with their start and end apart: 11, of which 4 were waited for; matrix products, arithmetic and copies ran while one was open for 0% of the time, Pallas kernels for 37%

profile of v3, /device:TPU:0, one launch (start us, length us, event | category | flops | bytes accessed | tf_op | source)
XLA Modules:
  0.0 36.9 jit_solution(5899403233612704175)
XLA Ops:
  0.0 0.0 copy-start
  0.0 0.0 copy-start.1
  0.0 3.0 %collective-permute-start = (f32[256,256]{1,0:T(8,128)}, f32[256,256]{1,0:T(8,128)S(1)}, u32[]{:S(2)}, u32[]{:S(2)}) collective-permute-start(f32[256,256]{1,0:T(8,128)} %refs_2_.1), channel_id=1, source_target_pairs={{0,8},{2,10},{4,12},{6,14},{8,0},{10,2},{12,4},{14,6},{16,24},{18,... | collective-permute-start | bytes 786440 | tf_op jit(solution)/shard_map/ppermute | solution.py:24
  3.0 1.5 %collective-permute-start.1 = (f32[256,256]{1,0:T(8,128)}, f32[256,256]{1,0:T(8,128)S(1)}, u32[]{:S(2)}, u32[]{:S(2)}) collective-permute-start(f32[256,256]{1,0:T(8,128)} %refs_2_.1), channel_id=1, source_target_pairs={{0,4},{2,6},{4,0},{6,2},{8,12},{10,14},{12,8},{14,10},{16,20},{18,... | collective-permute-start | bytes 786440 | tf_op jit(solution)/shard_map/ppermute | solution.py:24
  4.5 0.0 collective-permute-start.2
  4.6 6.8 %project.2 = (f32[8,64,128]{2,1,0:T(8,128)S(1)}, bf16[64,4096]{1,0:T(8,128)(2,1)S(1)}, bf16[64,14336]{1,0:T(8,128)(2,1)S(1)}, bf16[8,64,4096]{2,1,0:T(8,128)(2,1)S(1)}, bf16[8,64,14336]{2,1,0:T(8,128)(2,1)S(1)}) custom-call(s32[4]{0:T(128)} %lengths.3, bf16[1024,4096]{1,0:T(8,128)(2,1)} %acts.3, bf16[1024,14336]{1,0:T(8,128)(2,1)} %grads.3, ...), custom_call_target="tpu_custom_call" | custom-call | flops 1207959552 | bytes 18874368 | tf_op jit(solution)/shard_map/project/pallas_call | solution.py:170
  11.4 2.4 %collective-permute-start.3 = (f32[8,64,128]{2,1,0:T(8,128)S(1)}, f32[8,64,128]{2,1,0:T(8,128)S(1)}, u32[]{:S(2)}, u32[]{:S(2)}) collective-permute-start(f32[8,64,128]{2,1,0:T(8,128)S(1)} %get-tuple-element.28), channel_id=1, source_target_pairs={{0,1},{1,0},{2,3},{3,2},{4,5},{5,4},{6,7},{7,6},{8,9},{9,8},{10,11... | collective-permute-start | bytes 786440 | tf_op jit(solution)/shard_map/ppermute | solution.py:297
  13.8 0.0 copy-done
  13.8 0.0 collective-permute-start.5
  13.8 0.0 copy-done.1
  13.8 0.0 copy-start.2
  13.8 6.1 %project.3 = (f32[8,64,128]{2,1,0:T(8,128)S(1)}, bf16[8,64,4096]{2,1,0:T(8,128)(2,1)S(1)}, bf16[8,64,14336]{2,1,0:T(8,128)(2,1)S(1)}) custom-call(s32[4]{0:T(128)S(1)} %copy-done.1, bf16[1024,4096]{1,0:T(8,128)(2,1)} %acts.3, bf16[1024,14336]{1,0:T(8,128)(2,1)} %grads.3, ...), custom_call_target="tpu_custom_call", output_to_operand_aliasing={{1}: (5, {}), {2}: (6, {})} | custom-call | flops 1207959552 | bytes 18874368 | tf_op jit(solution)/shard_map/project/pallas_call | solution.py:170
  19.9 0.0 collective-permute-done.refs_6_
  19.9 0.0 collective-permute-done.1.refs_4_
  20.0 0.0 collective-permute-done.2.refs_3_
  20.0 0.2 collective-permute-done.3
  20.2 0.7 %units.1 = f32[2,2,8,256]{3,2,1,0:T(8,128)S(1)} custom-call(f32[2,256,128]{2,1,0:T(8,128)S(1)} %bitcast.7, f32[2,256,128]{2,1,0:T(8,128)S(1)} %bitcast.6), custom_call_target="tpu_custom_call" | custom-call | tf_op jit(solution)/shard_map/units/pallas_call | solution.py:221
  20.9 1.4 %collective-permute-start.4 = (f32[2,2,8,256]{3,2,1,0:T(8,128)S(1)}, f32[2,2,8,256]{3,2,1,0:T(8,128)S(1)}, u32[]{:S(2)}, u32[]{:S(2)}) collective-permute-start(f32[2,2,8,256]{3,2,1,0:T(8,128)S(1)} %units.1), channel_id=1, source_target_pairs={{0,1},{1,0},{2,3},{3,2},{4,5},{5,4},{6,7},{7,6},{8,9},{9,8},{10,11... | collective-permute-start | bytes 98312 | tf_op jit(solution)/shard_map/ppermute | solution.py:310
  22.2 0.0 collective-permute-start.7
  22.2 0.5 %collective-permute-start.8 = (f32[256,256]{1,0:T(8,128)S(1)}, f32[256,256]{1,0:T(8,128)S(1)}, u32[]{:S(2)}, u32[]{:S(2)}) collective-permute-start(f32[256,256]{1,0:T(8,128)S(1)} %collective-permute-done.refs_6_), channel_id=1, source_target_pairs={{0,2},{2,0},{4,6},{6,4},{8,10},{10,8},{12,14},{14,12},{16,18},{18,... | collective-permute-start | bytes 786440 | tf_op jit(solution)/shard_map/ppermute | solution.py:24
  22.7 2.1 %collective-permute-done.4 = f32[2,2,8,256]{3,2,1,0:T(8,128)S(1)} collective-permute-done((f32[2,2,8,256]{3,2,1,0:T(8,128)S(1)}, f32[2,2,8,256]{3,2,1,0:T(8,128)S(1)}, u32[]{:S(2)}, u32[]{:S(2)}) %collective-permute-start.4) | collective-permute-done | bytes 32800 | tf_op jit(solution)/shard_map/ppermute | solution.py:310
  24.8 0.0 collective-permute-done.5.refs_8_
  24.9 0.1 collective-permute-start.9
  24.9 4.1 %collective-permute-start.6 = (f32[4,8,256]{2,1,0:T(8,128)S(1)}, f32[4,8,256]{2,1,0:T(8,128)S(1)}, u32[]{:S(2)}, u32[]{:S(2)}) collective-permute-start(f32[4,8,256]{2,1,0:T(8,128)S(1)} %get-tuple-element.39), channel_id=1, source_target_pairs={{0,16},{2,18},{4,20},{6,22},{8,24},{10,26},{12,28},{14,30},{16,0},... | collective-permute-start | bytes 98312 | tf_op jit(solution)/shard_map/ppermute | solution.py:24
  29.0 2.0 %collective-permute-done.6.refs_1_ = f32[4,8,256]{2,1,0:T(8,128)S(1)} collective-permute-done((f32[4,8,256]{2,1,0:T(8,128)S(1)}, f32[4,8,256]{2,1,0:T(8,128)S(1)}, u32[]{:S(2)}, u32[]{:S(2)}) %collective-permute-start.6) | collective-permute-done | bytes 32800 | tf_op jit(solution)/shard_map/ppermute | solution.py:24
  31.0 0.0 collective-permute-done.7.refs_5_
  31.0 0.0 collective-permute-done.8.refs_7_
  31.0 0.0 collective-permute-done.9.refs_9_
  31.0 0.6 %scores.1 = (f32[4,256]{1,0:T(4,128)S(1)}, f32[4,256]{1,0:T(4,128)S(1)}) custom-call(f32[4,8,256]{2,1,0:T(8,128)S(1)} %get-tuple-element.40.refs_0_, f32[4,8,256]{2,1,0:T(8,128)S(1)} %collective-permute-done.6.refs_1_, f32[256,256]{1,0:T(8,128)S(1)} %copy-done, f32[256,256]{1,0:T(8,128)S(1)} %collective-permute-done.2.refs_3_, ...), custom_call_target="tpu_custom_call" | custom-call | tf_op jit(solution)/shard_map/scores/pallas_call | solution.py:263
  31.7 2.9 %collective-permute-start.10 = (f32[4,256]{1,0:T(4,128)S(1)}, f32[4,256]{1,0:T(4,128)S(1)}, u32[]{:S(2)}, u32[]{:S(2)}) collective-permute-start(f32[4,256]{1,0:T(4,128)S(1)} %get-tuple-element.38), channel_id=1, source_target_pairs={{0,16},{2,18},{4,20},{6,22},{8,24},{10,26},{12,28},{14,30},{16,0},... | collective-permute-start | bytes 12296 | tf_op jit(solution)/shard_map/ppermute | solution.py:24
  34.6 1.7 %collective-permute-done.10 = f32[4,256]{1,0:T(4,128)S(1)} collective-permute-done((f32[4,256]{1,0:T(4,128)S(1)}, f32[4,256]{1,0:T(4,128)S(1)}, u32[]{:S(2)}, u32[]{:S(2)}) %collective-permute-start.10) | collective-permute-done | bytes 4128 | tf_op jit(solution)/shard_map/ppermute | solution.py:24
  36.3 0.0 copy-done.2
  36.3 0.7 %add_select_fusion = f32[4,256]{1,0:T(4,128)} fusion(f32[4,256]{1,0:T(4,128)S(1)} %get-tuple-element.37, f32[4,256]{1,0:T(4,128)S(1)} %collective-permute-done.10, s32[256]{0:T(256)S(1)} %copy-done.2, s32[4]{0:T(128)S(1)} %iota_add_fusion), kind=kLoop, calls=%fused_computation.3 | loop fusion | flops 3072 | bytes 13328 | tf_op jit(solution)/shard_map/jit(_where)/select_n | solution.py:324
  (3 shorter events, 0.0 us)
Async XLA Ops:
  0.0 13.8 %copy-start = (f32[256,256]{1,0:T(8,128)S(1)}, f32[256,256]{1,0:T(8,128)}, u32[]{:S(2)}) copy-start(f32[256,256]{1,0:T(8,128)} %refs_2_.1) | copy-start | bytes 786436
  0.0 13.8 %copy-start.1 = (s32[4]{0:T(128)S(1)}, s32[4]{0:T(128)}, u32[]{:S(2)}) copy-start(s32[4]{0:T(128)} %lengths.3) | copy-start | bytes 52
  0.0 19.9 %collective-permute-start = (f32[256,256]{1,0:T(8,128)}, f32[256,256]{1,0:T(8,128)S(1)}, u32[]{:S(2)}, u32[]{:S(2)}) collective-permute-start(f32[256,256]{1,0:T(8,128)} %refs_2_.1), channel_id=1, source_target_pairs={{0,8},{2,10},{4,12},{6,14},{8,0},{10,2},{12,4},{14,6},{16,24},{18,... | collective-permute-start | bytes 786440 | tf_op jit(solution)/shard_map/ppermute | solution.py:24
  3.0 16.9 %collective-permute-start.1 = (f32[256,256]{1,0:T(8,128)}, f32[256,256]{1,0:T(8,128)S(1)}, u32[]{:S(2)}, u32[]{:S(2)}) collective-permute-start(f32[256,256]{1,0:T(8,128)} %refs_2_.1), channel_id=1, source_target_pairs={{0,4},{2,6},{4,0},{6,2},{8,12},{10,14},{12,8},{14,10},{16,20},{18,... | collective-permute-start | bytes 786440 | tf_op jit(solution)/shard_map/ppermute | solution.py:24
  4.5 15.4 %collective-permute-start.2 = (f32[256,256]{1,0:T(8,128)}, f32[256,256]{1,0:T(8,128)S(1)}, u32[]{:S(2)}, u32[]{:S(2)}) collective-permute-start(f32[256,256]{1,0:T(8,128)} %refs_2_.1), channel_id=1, source_target_pairs={{0,2},{2,0},{4,6},{6,4},{8,10},{10,8},{12,14},{14,12},{16,18},{18,... | collective-permute-start | bytes 786440 | tf_op jit(solution)/shard_map/ppermute | solution.py:24
  11.4 8.8 %collective-permute-start.3 = (f32[8,64,128]{2,1,0:T(8,128)S(1)}, f32[8,64,128]{2,1,0:T(8,128)S(1)}, u32[]{:S(2)}, u32[]{:S(2)}) collective-permute-start(f32[8,64,128]{2,1,0:T(8,128)S(1)} %get-tuple-element.28), channel_id=1, source_target_pairs={{0,1},{1,0},{2,3},{3,2},{4,5},{5,4},{6,7},{7,6},{8,9},{9,8},{10,11... | collective-permute-start | bytes 786440 | tf_op jit(solution)/shard_map/ppermute | solution.py:297
  13.8 11.1 %collective-permute-start.5 = (f32[256,256]{1,0:T(8,128)S(1)}, f32[256,256]{1,0:T(8,128)S(1)}, u32[]{:S(2)}, u32[]{:S(2)}) collective-permute-start(f32[256,256]{1,0:T(8,128)S(1)} %copy-done), channel_id=1, source_target_pairs={{0,12},{2,14},{4,8},{6,10},{8,4},{10,6},{12,0},{14,2},{16,28},{18,... | collective-permute-start | bytes 786440 | tf_op jit(solution)/shard_map/ppermute | solution.py:24
  13.8 22.5 %copy-start.2 = (s32[256]{0:T(256)S(1)}, s32[256]{0:T(256)}, u32[]{:S(2)}) copy-start(s32[256]{0:T(256)} %param.13) | copy-start | bytes 3076
  20.9 4.0 %collective-permute-start.4 = (f32[2,2,8,256]{3,2,1,0:T(8,128)S(1)}, f32[2,2,8,256]{3,2,1,0:T(8,128)S(1)}, u32[]{:S(2)}, u32[]{:S(2)}) collective-permute-start(f32[2,2,8,256]{3,2,1,0:T(8,128)S(1)} %units.1), channel_id=1, source_target_pairs={{0,1},{1,0},{2,3},{3,2},{4,5},{5,4},{6,7},{7,6},{8,9},{9,8},{10,11... | collective-permute-start | bytes 98312 | tf_op jit(solution)/shard_map/ppermute | solution.py:310
  22.2 8.8 %collective-permute-start.7 = (f32[256,256]{1,0:T(8,128)S(1)}, f32[256,256]{1,0:T(8,128)S(1)}, u32[]{:S(2)}, u32[]{:S(2)}) collective-permute-start(f32[256,256]{1,0:T(8,128)S(1)} %collective-permute-done.1.refs_4_), channel_id=1, source_target_pairs={{0,2},{2,0},{4,6},{6,4},{8,10},{10,8},{12,14},{14,12},{16,18},{18,... | collective-permute-start | bytes 786440 | tf_op jit(solution)/shard_map/ppermute | solution.py:24
  22.2 8.8 %collective-permute-start.8 = (f32[256,256]{1,0:T(8,128)S(1)}, f32[256,256]{1,0:T(8,128)S(1)}, u32[]{:S(2)}, u32[]{:S(2)}) collective-permute-start(f32[256,256]{1,0:T(8,128)S(1)} %collective-permute-done.refs_6_), channel_id=1, source_target_pairs={{0,2},{2,0},{4,6},{6,4},{8,10},{10,8},{12,14},{14,12},{16,18},{18,... | collective-permute-start | bytes 786440 | tf_op jit(solution)/shard_map/ppermute | solution.py:24
  24.9 6.2 %collective-permute-start.9 = (f32[256,256]{1,0:T(8,128)S(1)}, f32[256,256]{1,0:T(8,128)S(1)}, u32[]{:S(2)}, u32[]{:S(2)}) collective-permute-start(f32[256,256]{1,0:T(8,128)S(1)} %collective-permute-done.5.refs_8_), channel_id=1, source_target_pairs={{0,2},{2,0},{4,6},{6,4},{8,10},{10,8},{12,14},{14,12},{16,18},{18,... | collective-permute-start | bytes 786440 | tf_op jit(solution)/shard_map/ppermute | solution.py:24
  24.9 6.1 %collective-permute-start.6 = (f32[4,8,256]{2,1,0:T(8,128)S(1)}, f32[4,8,256]{2,1,0:T(8,128)S(1)}, u32[]{:S(2)}, u32[]{:S(2)}) collective-permute-start(f32[4,8,256]{2,1,0:T(8,128)S(1)} %get-tuple-element.39), channel_id=1, source_target_pairs={{0,16},{2,18},{4,20},{6,22},{8,24},{10,26},{12,28},{14,30},{16,0},... | collective-permute-start | bytes 98312 | tf_op jit(solution)/shard_map/ppermute | solution.py:24
  31.7 4.6 %collective-permute-start.10 = (f32[4,256]{1,0:T(4,128)S(1)}, f32[4,256]{1,0:T(4,128)S(1)}, u32[]{:S(2)}, u32[]{:S(2)}) collective-permute-start(f32[4,256]{1,0:T(4,128)S(1)} %get-tuple-element.38), channel_id=1, source_target_pairs={{0,16},{2,18},{4,20},{6,22},{8,24},{10,26},{12,28},{14,30},{16,0},... | collective-permute-start | bytes 12296 | tf_op jit(solution)/shard_map/ppermute | solution.py:24

commit v4 on v3

--- a/solution.py
+++ b/solution.py
@@ -289,7 +289,7 @@
     args = (lengths, acts, out_grads, proj_in, proj_out)
     blocks = {0: queries}
     for m in near:
-        if m == 1 or m % 2 == 0 and m > 0:
+        if m % 2 == 0 and m > 0:
             blocks[m] = swap(queries, m)
     if halves:
         count = ex_count // 2
@@ -299,19 +299,19 @@
     else:
         count = ex_count
         parts = [lax.psum(project(None, count, slot, *args)[0], "tensor")]
-    early = [m for m in reversed(bits[:NEAR_BITS])]
+    early = [m for m in reversed(bits[1:NEAR_BITS])]
     held, parts[0] = lax.optimization_barrier(([blocks[m] for m in early], parts[0]))
     blocks.update(zip(early, held))
     own = units(parts, count, slot, rank_out, split, near, rest)
-    own, held = lax.optimization_barrier((own, [blocks[m] for m in bits[1:NEAR_BITS]]))
-    blocks.update(zip(bits[1:NEAR_BITS], held))
+    own, held = lax.optimization_barrier((own, [blocks[m] for m in (0, *early)]))
+    blocks.update(zip((0, *early), held))
     last = near[-1] ^ 1
     if halves:
         own = jnp.concatenate([own, lax.ppermute(own, "tensor", [(0, 1), (1, 0)])], axis=1)
         own, blocks[last] = lax.optimization_barrier((own, blocks[last]))
     rows_of = [own[g] if r == 0 else swap(own[g], r) for g, r in enumerate(rest)]
     for m in near:
-        if m > 1 and m % 2 == 1:
+        if m % 2 == 1:
             blocks[m] = swap(blocks[m ^ 1], 1)
     sums = partial_scores(rows_of, [blocks[m] for m in near], halves)
     scores = sums[0]

time: 37.5 us -> 36.9 us (0.984); the launches traced: 36.9 us -> 36.9 us
  waiting for transfers between devices: 5.97 us -> 7.42 us
  Pallas kernels: 14.3 us -> 13.2 us
  starting transfers between devices: 15.9 us -> 15.5 us
    ppermute x9, waiting for transfers between devices: 3.66 us -> 6.8 us  [swap(): return lax.ppermute(x, 'dp', xor_pairs(lax.axis_size('dp'), mask))]
    ppermute x1, waiting for transfers between devices: 2.12 us -> 0.62 us  [on_device(): lax.ppermute(own, 'tensor', [(0, 1), (1, 0)])]
    pallas_call x2, Pallas kernels: 13 us -> 11.8 us  [project(): pl.pallas_call(functools.partial(project_kernel, peer, count, slot, bool(...]
    ppermute x1, starting transfers between devices: 1.35 us -> 1.95 us  [on_device(): lax.ppermute(own, 'tensor', [(0, 1), (1, 0)])]
    ppermute x1, starting transfers between devices: 2.38 us -> 1.88 us  [on_device(): arrived = lax.ppermute(theirs, 'tensor', [(0, 1), (1, 0)])]
    ppermute x9, starting transfers between devices: 12.1 us -> 11.7 us  [swap(): return lax.ppermute(x, 'dp', xor_pairs(lax.axis_size('dp'), mask))]
  transfers between devices with their start and end apart: 11 -> 11, of which waited for: 4 -> 3; matrix products, arithmetic and copies ran while one was open for 0% -> 0% of each run, Pallas kernels for 37% -> 34%
where the time goes in v4:
time: 36.9 us
  starting transfers between devices  15.5 us (42%)
  Pallas kernels  13.2 us (36%)
  waiting for transfers between devices  7.42 us (20%)
  other arithmetic  0.67 us (2%)
    pallas_call x2, Pallas kernels, project(): pl.pallas_call(functools.partial(project_kernel, peer, count, slot, bool(...  11.8 us
    ppermute x9, starting transfers between devices, swap(): return lax.ppermute(x, 'dp', xor_pairs(lax.axis_size('dp'), mask))  11.7 us
    ppermute x9, waiting for transfers between devices, swap(): return lax.ppermute(x, 'dp', xor_pairs(lax.axis_size('dp'), mask))  6.8 us
    ppermute x1, starting transfers between devices, on_device(): lax.ppermute(own, 'tensor', [(0, 1), (1, 0)])  1.95 us
    ppermute x1, starting transfers between devices, on_device(): arrived = lax.ppermute(theirs, 'tensor', [(0, 1), (1, 0)])  1.88 us
  transfers between devices with their start and end apart: 11, of which 3 were waited for; matrix products, arithmetic and copies ran while one was open for 0% of the time, Pallas kernels for 34%

profile of v4, /device:TPU:0, one launch (start us, length us, event | category | flops | bytes accessed | tf_op | source)
XLA Modules:
  0.0 36.9 jit_solution(326080525006711075)
XLA Ops:
  0.0 0.0 copy-start
  0.0 0.0 copy-start.1
  0.0 3.0 %collective-permute-start = (f32[256,256]{1,0:T(8,128)}, f32[256,256]{1,0:T(8,128)S(1)}, u32[]{:S(2)}, u32[]{:S(2)}) collective-permute-start(f32[256,256]{1,0:T(8,128)} %refs_2_), channel_id=1, source_target_pairs={{0,8},{2,10},{4,12},{6,14},{8,0},{10,2},{12,4},{14,6},{16,24},{18,... | collective-permute-start | bytes 786440 | tf_op jit(solution)/shard_map/ppermute | solution.py:24
  3.0 1.5 %collective-permute-start.1 = (f32[256,256]{1,0:T(8,128)}, f32[256,256]{1,0:T(8,128)S(1)}, u32[]{:S(2)}, u32[]{:S(2)}) collective-permute-start(f32[256,256]{1,0:T(8,128)} %refs_2_), channel_id=1, source_target_pairs={{0,4},{2,6},{4,0},{6,2},{8,12},{10,14},{12,8},{14,10},{16,20},{18,... | collective-permute-start | bytes 786440 | tf_op jit(solution)/shard_map/ppermute | solution.py:24
  4.5 6.5 %project.2 = (f32[8,64,128]{2,1,0:T(8,128)S(1)}, bf16[64,4096]{1,0:T(8,128)(2,1)S(1)}, bf16[64,14336]{1,0:T(8,128)(2,1)S(1)}, bf16[8,64,4096]{2,1,0:T(8,128)(2,1)S(1)}, bf16[8,64,14336]{2,1,0:T(8,128)(2,1)S(1)}) custom-call(s32[4]{0:T(128)} %lengths.3, bf16[1024,4096]{1,0:T(8,128)(2,1)} %acts.3, bf16[1024,14336]{1,0:T(8,128)(2,1)} %grads.3, ...), custom_call_target="tpu_custom_call" | custom-call | flops 1207959552 | bytes 18874368 | tf_op jit(solution)/shard_map/project/pallas_call | solution.py:170
  11.1 1.9 %collective-permute-start.2 = (f32[8,64,128]{2,1,0:T(8,128)S(1)}, f32[8,64,128]{2,1,0:T(8,128)S(1)}, u32[]{:S(2)}, u32[]{:S(2)}) collective-permute-start(f32[8,64,128]{2,1,0:T(8,128)S(1)} %get-tuple-element.28), channel_id=1, source_target_pairs={{0,1},{1,0},{2,3},{3,2},{4,5},{5,4},{6,7},{7,6},{8,9},{9,8},{10,11... | collective-permute-start | bytes 786440 | tf_op jit(solution)/shard_map/ppermute | solution.py:297
  12.9 0.0 copy-done
  12.9 1.2 %collective-permute-start.4 = (f32[256,256]{1,0:T(8,128)S(1)}, f32[256,256]{1,0:T(8,128)S(1)}, u32[]{:S(2)}, u32[]{:S(2)}) collective-permute-start(f32[256,256]{1,0:T(8,128)S(1)} %copy-done), channel_id=1, source_target_pairs={{0,12},{2,14},{4,8},{6,10},{8,4},{10,6},{12,0},{14,2},{16,28},{18,... | collective-permute-start | bytes 786440 | tf_op jit(solution)/shard_map/ppermute | solution.py:24
  14.1 0.0 copy-done.1
  14.1 0.0 copy-start.2
  14.2 5.3 %project.3 = (f32[8,64,128]{2,1,0:T(8,128)S(1)}, bf16[8,64,4096]{2,1,0:T(8,128)(2,1)S(1)}, bf16[8,64,14336]{2,1,0:T(8,128)(2,1)S(1)}) custom-call(s32[4]{0:T(128)S(1)} %copy-done.1, bf16[1024,4096]{1,0:T(8,128)(2,1)} %acts.3, bf16[1024,14336]{1,0:T(8,128)(2,1)} %grads.3, ...), custom_call_target="tpu_custom_call", output_to_operand_aliasing={{1}: (5, {}), {2}: (6, {})} | custom-call | flops 1207959552 | bytes 18874368 | tf_op jit(solution)/shard_map/project/pallas_call | solution.py:170
  19.5 0.0 collective-permute-done.refs_6_
  19.5 0.0 collective-permute-done.1.refs_4_
  19.5 0.0 collective-permute-done.2
  19.5 0.7 %units.1 = f32[2,2,8,256]{3,2,1,0:T(8,128)S(1)} custom-call(f32[2,256,128]{2,1,0:T(8,128)S(1)} %bitcast.7, f32[2,256,128]{2,1,0:T(8,128)S(1)} %bitcast.6), custom_call_target="tpu_custom_call" | custom-call | tf_op jit(solution)/shard_map/units/pallas_call | solution.py:221
  20.2 1.9 %collective-permute-start.3 = (f32[2,2,8,256]{3,2,1,0:T(8,128)S(1)}, f32[2,2,8,256]{3,2,1,0:T(8,128)S(1)}, u32[]{:S(2)}, u32[]{:S(2)}) collective-permute-start(f32[2,2,8,256]{3,2,1,0:T(8,128)S(1)} %units.1), channel_id=1, source_target_pairs={{0,1},{1,0},{2,3},{3,2},{4,5},{5,4},{6,7},{7,6},{8,9},{9,8},{10,11... | collective-permute-start | bytes 98312 | tf_op jit(solution)/shard_map/ppermute | solution.py:310
  22.2 0.9 %collective-permute-start.6 = (f32[256,256]{1,0:T(8,128)S(1)}, f32[256,256]{1,0:T(8,128)S(1)}, u32[]{:S(2)}, u32[]{:S(2)}) collective-permute-start(f32[256,256]{1,0:T(8,128)S(1)} %copy-done), channel_id=1, source_target_pairs={{0,2},{2,0},{4,6},{6,4},{8,10},{10,8},{12,14},{14,12},{16,18},{18,... | collective-permute-start | bytes 786440 | tf_op jit(solution)/shard_map/ppermute | solution.py:24
  23.1 0.1 collective-permute-start.7
  23.1 0.4 %collective-permute-start.8 = (f32[256,256]{1,0:T(8,128)S(1)}, f32[256,256]{1,0:T(8,128)S(1)}, u32[]{:S(2)}, u32[]{:S(2)}) collective-permute-start(f32[256,256]{1,0:T(8,128)S(1)} %collective-permute-done.refs_6_), channel_id=1, source_target_pairs={{0,2},{2,0},{4,6},{6,4},{8,10},{10,8},{12,14},{14,12},{16,18},{18,... | collective-permute-start | bytes 786440 | tf_op jit(solution)/shard_map/ppermute | solution.py:24
  23.6 0.6 %collective-permute-done.3 = f32[2,2,8,256]{3,2,1,0:T(8,128)S(1)} collective-permute-done((f32[2,2,8,256]{3,2,1,0:T(8,128)S(1)}, f32[2,2,8,256]{3,2,1,0:T(8,128)S(1)}, u32[]{:S(2)}, u32[]{:S(2)}) %collective-permute-start.3) | collective-permute-done | bytes 32800 | tf_op jit(solution)/shard_map/ppermute | solution.py:310
  24.2 0.0 collective-permute-done.4.refs_8_
  24.2 1.6 %collective-permute-start.9 = (f32[256,256]{1,0:T(8,128)S(1)}, f32[256,256]{1,0:T(8,128)S(1)}, u32[]{:S(2)}, u32[]{:S(2)}) collective-permute-start(f32[256,256]{1,0:T(8,128)S(1)} %collective-permute-done.4.refs_8_), channel_id=1, source_target_pairs={{0,2},{2,0},{4,6},{6,4},{8,10},{10,8},{12,14},{14,12},{16,18},{18,... | collective-permute-start | bytes 786440 | tf_op jit(solution)/shard_map/ppermute | solution.py:24
  25.8 1.6 %collective-permute-start.5 = (f32[4,8,256]{2,1,0:T(8,128)S(1)}, f32[4,8,256]{2,1,0:T(8,128)S(1)}, u32[]{:S(2)}, u32[]{:S(2)}) collective-permute-start(f32[4,8,256]{2,1,0:T(8,128)S(1)} %get-tuple-element.39), channel_id=1, source_target_pairs={{0,16},{2,18},{4,20},{6,22},{8,24},{10,26},{12,28},{14,30},{16,0},... | collective-permute-start | bytes 98312 | tf_op jit(solution)/shard_map/ppermute | solution.py:24
  27.4 3.6 %collective-permute-done.5.refs_1_ = f32[4,8,256]{2,1,0:T(8,128)S(1)} collective-permute-done((f32[4,8,256]{2,1,0:T(8,128)S(1)}, f32[4,8,256]{2,1,0:T(8,128)S(1)}, u32[]{:S(2)}, u32[]{:S(2)}) %collective-permute-start.5) | collective-permute-done | bytes 32800 | tf_op jit(solution)/shard_map/ppermute | solution.py:24
  31.0 0.0 collective-permute-done.6.refs_3_
  31.0 0.0 collective-permute-done.7.refs_5_
  31.0 0.0 collective-permute-done.8.refs_7_
  31.0 0.0 collective-permute-done.9.refs_9_
  31.0 0.6 %scores.1 = (f32[4,256]{1,0:T(4,128)S(1)}, f32[4,256]{1,0:T(4,128)S(1)}) custom-call(f32[4,8,256]{2,1,0:T(8,128)S(1)} %get-tuple-element.40.refs_0_, f32[4,8,256]{2,1,0:T(8,128)S(1)} %collective-permute-done.5.refs_1_, f32[256,256]{1,0:T(8,128)S(1)} %copy-done, f32[256,256]{1,0:T(8,128)S(1)} %collective-permute-done.6.refs_3_, ...), custom_call_target="tpu_custom_call" | custom-call | tf_op jit(solution)/shard_map/scores/pallas_call | solution.py:263
  31.6 1.3 %collective-permute-start.10 = (f32[4,256]{1,0:T(4,128)S(1)}, f32[4,256]{1,0:T(4,128)S(1)}, u32[]{:S(2)}, u32[]{:S(2)}) collective-permute-start(f32[4,256]{1,0:T(4,128)S(1)} %get-tuple-element.38), channel_id=1, source_target_pairs={{0,16},{2,18},{4,20},{6,22},{8,24},{10,26},{12,28},{14,30},{16,0},... | collective-permute-start | bytes 12296 | tf_op jit(solution)/shard_map/ppermute | solution.py:24
  33.0 3.2 %collective-permute-done.10 = f32[4,256]{1,0:T(4,128)S(1)} collective-permute-done((f32[4,256]{1,0:T(4,128)S(1)}, f32[4,256]{1,0:T(4,128)S(1)}, u32[]{:S(2)}, u32[]{:S(2)}) %collective-permute-start.10) | collective-permute-done | bytes 4128 | tf_op jit(solution)/shard_map/ppermute | solution.py:24
  36.2 0.0 copy-done.2
  36.2 0.7 %add_select_fusion = f32[4,256]{1,0:T(4,128)} fusion(f32[4,256]{1,0:T(4,128)S(1)} %get-tuple-element.37, f32[4,256]{1,0:T(4,128)S(1)} %collective-permute-done.10, s32[256]{0:T(256)S(1)} %copy-done.2, s32[4]{0:T(128)S(1)} %iota_add_fusion), kind=kLoop, calls=%fused_computation.3 | loop fusion | flops 3072 | bytes 13328 | tf_op jit(solution)/shard_map/jit(_where)/select_n | solution.py:324
  (3 shorter events, 0.0 us)
Async XLA Ops:
  0.0 12.9 %copy-start = (f32[256,256]{1,0:T(8,128)S(1)}, f32[256,256]{1,0:T(8,128)}, u32[]{:S(2)}) copy-start(f32[256,256]{1,0:T(8,128)} %refs_2_) | copy-start | bytes 786436
  0.0 14.1 %copy-start.1 = (s32[4]{0:T(128)S(1)}, s32[4]{0:T(128)}, u32[]{:S(2)}) copy-start(s32[4]{0:T(128)} %lengths.3) | copy-start | bytes 52
  0.0 19.5 %collective-permute-start = (f32[256,256]{1,0:T(8,128)}, f32[256,256]{1,0:T(8,128)S(1)}, u32[]{:S(2)}, u32[]{:S(2)}) collective-permute-start(f32[256,256]{1,0:T(8,128)} %refs_2_), channel_id=1, source_target_pairs={{0,8},{2,10},{4,12},{6,14},{8,0},{10,2},{12,4},{14,6},{16,24},{18,... | collective-permute-start | bytes 786440 | tf_op jit(solution)/shard_map/ppermute | solution.py:24
  3.0 16.5 %collective-permute-start.1 = (f32[256,256]{1,0:T(8,128)}, f32[256,256]{1,0:T(8,128)S(1)}, u32[]{:S(2)}, u32[]{:S(2)}) collective-permute-start(f32[256,256]{1,0:T(8,128)} %refs_2_), channel_id=1, source_target_pairs={{0,4},{2,6},{4,0},{6,2},{8,12},{10,14},{12,8},{14,10},{16,20},{18,... | collective-permute-start | bytes 786440 | tf_op jit(solution)/shard_map/ppermute | solution.py:24
  11.1 8.5 %collective-permute-start.2 = (f32[8,64,128]{2,1,0:T(8,128)S(1)}, f32[8,64,128]{2,1,0:T(8,128)S(1)}, u32[]{:S(2)}, u32[]{:S(2)}) collective-permute-start(f32[8,64,128]{2,1,0:T(8,128)S(1)} %get-tuple-element.28), channel_id=1, source_target_pairs={{0,1},{1,0},{2,3},{3,2},{4,5},{5,4},{6,7},{7,6},{8,9},{9,8},{10,11... | collective-permute-start | bytes 786440 | tf_op jit(solution)/shard_map/ppermute | solution.py:297
  12.9 11.3 %collective-permute-start.4 = (f32[256,256]{1,0:T(8,128)S(1)}, f32[256,256]{1,0:T(8,128)S(1)}, u32[]{:S(2)}, u32[]{:S(2)}) collective-permute-start(f32[256,256]{1,0:T(8,128)S(1)} %copy-done), channel_id=1, source_target_pairs={{0,12},{2,14},{4,8},{6,10},{8,4},{10,6},{12,0},{14,2},{16,28},{18,... | collective-permute-start | bytes 786440 | tf_op jit(solution)/shard_map/ppermute | solution.py:24
  14.1 22.1 %copy-start.2 = (s32[256]{0:T(256)S(1)}, s32[256]{0:T(256)}, u32[]{:S(2)}) copy-start(s32[256]{0:T(256)} %param.13) | copy-start | bytes 3076
  20.2 4.0 %collective-permute-start.3 = (f32[2,2,8,256]{3,2,1,0:T(8,128)S(1)}, f32[2,2,8,256]{3,2,1,0:T(8,128)S(1)}, u32[]{:S(2)}, u32[]{:S(2)}) collective-permute-start(f32[2,2,8,256]{3,2,1,0:T(8,128)S(1)} %units.1), channel_id=1, source_target_pairs={{0,1},{1,0},{2,3},{3,2},{4,5},{5,4},{6,7},{7,6},{8,9},{9,8},{10,11... | collective-permute-start | bytes 98312 | tf_op jit(solution)/shard_map/ppermute | solution.py:310
  22.2 8.8 %collective-permute-start.6 = (f32[256,256]{1,0:T(8,128)S(1)}, f32[256,256]{1,0:T(8,128)S(1)}, u32[]{:S(2)}, u32[]{:S(2)}) collective-permute-start(f32[256,256]{1,0:T(8,128)S(1)} %copy-done), channel_id=1, source_target_pairs={{0,2},{2,0},{4,6},{6,4},{8,10},{10,8},{12,14},{14,12},{16,18},{18,... | collective-permute-start | bytes 786440 | tf_op jit(solution)/shard_map/ppermute | solution.py:24
  23.1 7.9 %collective-permute-start.7 = (f32[256,256]{1,0:T(8,128)S(1)}, f32[256,256]{1,0:T(8,128)S(1)}, u32[]{:S(2)}, u32[]{:S(2)}) collective-permute-start(f32[256,256]{1,0:T(8,128)S(1)} %collective-permute-done.1.refs_4_), channel_id=1, source_target_pairs={{0,2},{2,0},{4,6},{6,4},{8,10},{10,8},{12,14},{14,12},{16,18},{18,... | collective-permute-start | bytes 786440 | tf_op jit(solution)/shard_map/ppermute | solution.py:24
  23.1 7.8 %collective-permute-start.8 = (f32[256,256]{1,0:T(8,128)S(1)}, f32[256,256]{1,0:T(8,128)S(1)}, u32[]{:S(2)}, u32[]{:S(2)}) collective-permute-start(f32[256,256]{1,0:T(8,128)S(1)} %collective-permute-done.refs_6_), channel_id=1, source_target_pairs={{0,2},{2,0},{4,6},{6,4},{8,10},{10,8},{12,14},{14,12},{16,18},{18,... | collective-permute-start | bytes 786440 | tf_op jit(solution)/shard_map/ppermute | solution.py:24
  24.2 6.8 %collective-permute-start.9 = (f32[256,256]{1,0:T(8,128)S(1)}, f32[256,256]{1,0:T(8,128)S(1)}, u32[]{:S(2)}, u32[]{:S(2)}) collective-permute-start(f32[256,256]{1,0:T(8,128)S(1)} %collective-permute-done.4.refs_8_), channel_id=1, source_target_pairs={{0,2},{2,0},{4,6},{6,4},{8,10},{10,8},{12,14},{14,12},{16,18},{18,... | collective-permute-start | bytes 786440 | tf_op jit(solution)/shard_map/ppermute | solution.py:24
  25.8 5.1 %collective-permute-start.5 = (f32[4,8,256]{2,1,0:T(8,128)S(1)}, f32[4,8,256]{2,1,0:T(8,128)S(1)}, u32[]{:S(2)}, u32[]{:S(2)}) collective-permute-start(f32[4,8,256]{2,1,0:T(8,128)S(1)} %get-tuple-element.39), channel_id=1, source_target_pairs={{0,16},{2,18},{4,20},{6,22},{8,24},{10,26},{12,28},{14,30},{16,0},... | collective-permute-start | bytes 98312 | tf_op jit(solution)/shard_map/ppermute | solution.py:24
  31.6 4.6 %collective-permute-start.10 = (f32[4,256]{1,0:T(4,128)S(1)}, f32[4,256]{1,0:T(4,128)S(1)}, u32[]{:S(2)}, u32[]{:S(2)}) collective-permute-start(f32[4,256]{1,0:T(4,128)S(1)} %get-tuple-element.38), channel_id=1, source_target_pairs={{0,16},{2,18},{4,20},{6,22},{8,24},{10,26},{12,28},{14,30},{16,0},... | collective-permute-start | bytes 12296 | tf_op jit(solution)/shard_map/ppermute | solution.py:24
